TPU v7x, 256 devices: a whole 4x4x8 slice. The times are simulated.
256 devices in a mesh: side: 2 (over z_hi), brick: 128 (over z_lo, x, y, core).
Axes of the slice: x: 4, y: 4, z: 8 (z_hi: 2, z_lo: 4; z = z_hi * 4 + z_lo), core: 2. Of those that a mesh axis runs over, the one named last changes fastest.
Arguments:
- fields: float32 [10, 128, 256, 256], P('side', 'brick'), may hold values from -6 to 6
- source_field: float32 [128, 256, 256], P('brick'), may hold values from -6 to 6
- params_a: float32 [8], replicated, may hold values from 0 to 1
- params_b: float32 [8], replicated, may hold values from 0 to 1
- running_means: float32 [10, 128, 256, 256], P(None, None, ('side', 'brick')), may hold values from -6 to 6
- running_squares: float32 [10, 128, 256, 256], P(None, None, ('side', 'brick')), as said below
- running_cross: float32 [16, 128, 256, 256], P(None, None, ('side', 'brick')), as said below
Outputs:
- new_means: float32 [10, 128, 256, 256], P(None, None, ('side', 'brick'))
- new_squares: float32 [10, 128, 256, 256], P(None, None, ('side', 'brick'))
- new_cross: float32 [16, 128, 256, 256], P(None, None, ('side', 'brick'))
- sobol_maps: float32 [16, 128, 256, 256], P(None, None, ('side', 'brick'))
Inputs may be any that keep to these rules, and one draw needn't show every extreme that they name: `running_squares`: Positive. `running_cross`: each entry lies within 0.8 sqrt of the product of the two members' running_squares in magnitude.
All inputs are finite; a program needn't handle non-finite values.
Results may differ from a plain program's by a relative error of at most 0.00002.
Values sent between devices are 32-bit elements; how exact they have to be, the bound alone decides.
No kernel may reach another device: no remote copies, remote signals or barrier semaphores. Data moves between devices by JAX's collectives and lax.ppermute only.
A program may use at most 64 MiB of HBM per device.

v0:
```python
import jax
import jax.numpy as jnp
from jax import lax
from jax.sharding import PartitionSpec as P

PRIOR = 3


lower_bounds = (0.02, 0.02, 0.02, 0.01, 0.0, 0.0, 0.5, 0.0)
upper_bounds = (0.12, 0.12, 0.12, 0.06, 0.2, 1.0, 1.5, 0.1)


def with_halo(x, sides, width):
    for axis, dim in sides:
        peers, length = (lax.axis_size(axis), x.shape[dim])
        up = [(i, (i + 1) % peers) for i in range(peers - 1)]
        down = [(j, i) for i, j in up]
        last = lax.slice_in_dim(x, length - width, length, axis=dim)
        initial = lax.slice_in_dim(x, 0, width, axis=dim)
        before = lax.ppermute(last, axis, up)
        after = lax.ppermute(initial, axis, down)
        x = jnp.concatenate([before, x, after], axis=dim)
    return x


def swapped(block, axis, bit):
    count = lax.axis_size(axis)
    route = []
    for low in range(count):
        high = low | 1 << bit
        if high != low and high < count:
            route += [(low, high), (high, low)]
    return lax.ppermute(block, axis, route)


def member_theta(members, params_a, params_b):
    column = jnp.arange(params_a.shape[0], dtype=jnp.int32)
    from_b = (members[:, None] == 1) | (members[:, None] == column[None, :] + 2)
    unit = jnp.where(from_b, params_b[None, :], params_a[None, :])
    lower = jnp.asarray(lower_bounds, dtype=params_a.dtype)
    upper = jnp.asarray(upper_bounds, dtype=params_a.dtype)
    return lower[None, :] + (upper - lower)[None, :] * unit


def column_of(physical, index):
    return physical[:, index][:, None, None, None]


def stencil_update(
    current,
    physical,
    source_field,
    upwind_a,
    downwind_a,
    upwind_b,
    downwind_b,
    upwind_c,
    downwind_c,
):
    drift_first = column_of(physical, 0)
    drift_second = column_of(physical, 1)
    drift_third = column_of(physical, 2)
    diffusion = column_of(physical, 3)
    decay_rate = column_of(physical, 4)
    amplitude = column_of(physical, 5)
    anisotropy = column_of(physical, 6)
    reaction = column_of(physical, 7)
    laplace = (
        upwind_a
        + downwind_a
        + upwind_b
        + downwind_b
        + anisotropy * (upwind_c + downwind_c)
        - (4.0 + 2.0 * anisotropy) * current
    )
    change = (
        -drift_first * (current - upwind_a)
        - drift_second * (current - upwind_b)
        - drift_third * (current - upwind_c)
    )
    change = (
        change + diffusion * laplace - decay_rate * current - reaction * current * jnp.abs(current)
    )
    change = change + amplitude * source_field[None]
    return current + change


def advance(current, physical, source_field):
    widened = with_halo(current, (("brick", 1),), 1)
    padded = jnp.pad(current, ((0, 0), (0, 0), (1, 1), (1, 1)))
    return stencil_update(
        current,
        physical,
        source_field,
        widened[:, :-2],
        widened[:, 2:],
        padded[:, :, :-2, 1:-1],
        padded[:, :, 2:, 1:-1],
        padded[:, :, 1:-1, :-2],
        padded[:, :, 1:-1, 2:],
    )


def accumulate(outputs, running_means, running_squares, running_cross):
    total_count = float(PRIOR + 1)
    deviation = outputs - running_means
    new_means = running_means + deviation / total_count
    after = outputs - new_means
    new_squares = running_squares + deviation * after
    count_params = running_cross.shape[0] // 2
    first_cross = running_cross[:count_params] + deviation[1:2] * after[2:]
    total_cross = running_cross[count_params:] + deviation[0:1] * after[2:]
    new_cross = jnp.concatenate([first_cross, total_cross], axis=0)
    first_index = first_cross / jnp.sqrt(new_squares[1:2] * new_squares[2:])
    total_index = 1.0 - total_cross / jnp.sqrt(new_squares[0:1] * new_squares[2:])
    sobol_maps = jnp.concatenate([first_index, total_index], axis=0)
    return (new_means, new_squares, new_cross, sobol_maps)


def body(fields, source_field, params_a, params_b, running_means, running_squares, running_cross):
    local_count = fields.shape[0]
    side_index = lax.axis_index("side")
    members = side_index * local_count + jnp.arange(local_count, dtype=jnp.int32)
    physical = member_theta(members, params_a, params_b)
    current = advance(fields, physical, source_field)
    current = advance(current, physical, source_field)
    half_rows = current.shape[2] // 2
    kept_start = side_index * half_rows
    sent_start = (1 - side_index) * half_rows
    kept = lax.dynamic_slice_in_dim(current, kept_start, half_rows, 2)
    outgoing = lax.dynamic_slice_in_dim(current, sent_start, half_rows, 2)
    incoming = swapped(outgoing, "side", 0)
    lower_members = jnp.where(side_index == 0, kept, incoming)
    upper_members = jnp.where(side_index == 0, incoming, kept)
    mine = jnp.concatenate([lower_members, upper_members], axis=0)
    gathered = lax.all_to_all(mine, "brick", split_axis=2, concat_axis=1, tiled=True)
    return accumulate(gathered, running_means, running_squares, running_cross)


def solution(mesh):
    return jax.shard_map(
        body,
        mesh=mesh,
        in_specs=(
            P("side", "brick", None, None),
            P("brick", None, None),
            P(),
            P(),
            P(None, None, ("side", "brick"), None),
            P(None, None, ("side", "brick"), None),
            P(None, None, ("side", "brick"), None),
        ),
        out_specs=(
            P(None, None, ("side", "brick"), None),
            P(None, None, ("side", "brick"), None),
            P(None, None, ("side", "brick"), None),
            P(None, None, ("side", "brick"), None),
        ),
        check_vma=False,
    )
```

profile of v0, /device:TPU:1, one launch (start us, length us, event | category | flops | bytes accessed | tf_op | source)
XLA Modules:
  0.0 172.3 jit_solution(12999351311294496443)
XLA Ops:
  0.6 0.0 copy-start.5
  0.6 0.0 copy-start.6
  0.7 0.0 copy-start.4
  0.7 0.0 copy-start.3
  0.7 0.0 copy-start.2
  0.7 2.7 %copy.54 = f32[5,1,256,256]{3,1,0,2:T(1,128)S(1)} copy(f32[5,1,256,256]{3,2,1,0:T(8,128)} %param.9) | data formatting | bytes 2621440 | tf_op args[0]
  3.4 4.6 %collective-permute-start = (f32[5,1,256,256]{3,1,0,2:T(1,128)S(1)}, f32[5,1,256,256]{3,1,0,2:T(1,128)S(1)}, u32[]{:S(2)}, u32[]{:S(2)}) collective-permute-start(f32[5,1,256,256]{3,1,0,2:T(1,128)S(1)} %copy.54), channel_id=1, source_target_pairs={{0,1},{1,2},{2,3},{3,4},{4,5},{5,6},{6,7},{7,8},{8,9},{9,10},{10,1... | collective-permute-start | bytes 3932168 | tf_op jit(solution)/shard_map/ppermute | solution.py:20
  8.0 1.9 %collective-permute-start.1 = (f32[5,1,256,256]{3,1,0,2:T(1,128)S(1)}, f32[5,1,256,256]{3,1,0,2:T(1,128)}, u32[]{:S(2)}, u32[]{:S(2)}) collective-permute-start(f32[5,1,256,256]{3,1,0,2:T(1,128)S(1)} %copy.54), channel_id=1, source_target_pairs={{1,0},{2,1},{3,2},{4,3},{5,4},{6,5},{7,6},{8,7},{9,8},{10,9},{11,1... | collective-permute-start | bytes 3932168 | tf_op jit(solution)/shard_map/ppermute | solution.py:21
  10.0 0.0 copy-done.5
  10.0 0.0 copy-done.6
  10.0 0.0 copy-done.4
  10.0 0.0 copy-done.3
  10.0 0.1 multiply_add_fusion.3
  10.1 12.4 %collective-permute-done = f32[5,1,256,256]{3,1,0,2:T(1,128)S(1)} collective-permute-done((f32[5,1,256,256]{3,1,0,2:T(1,128)S(1)}, f32[5,1,256,256]{3,1,0,2:T(1,128)S(1)}, u32[]{:S(2)}, u32[]{:S(2)}) %collective-permute-start) | collective-permute-done | bytes 1310752 | tf_op jit(solution)/shard_map/ppermute | solution.py:20
  22.5 0.0 copy-start
  22.5 4.5 %collective-permute-done.1 = f32[5,1,256,256]{3,1,0,2:T(1,128)} collective-permute-done((f32[5,1,256,256]{3,1,0,2:T(1,128)S(1)}, f32[5,1,256,256]{3,1,0,2:T(1,128)}, u32[]{:S(2)}, u32[]{:S(2)}) %collective-permute-start.1) | collective-permute-done | bytes 1310752 | tf_op jit(solution)/shard_map/ppermute | solution.py:21
  27.0 0.0 copy-done
  27.0 0.0 copy-done.2
  27.0 12.0 %fusion = f32[5,1,256,256]{3,1,0,2:T(1,128)S(1)} fusion(f32[5,1,256,256]{3,1,0,2:T(1,128)S(1)} %copy.54, f32[5,1,256,256]{3,1,0,2:T(1,128)} %copy-done, f32[5,1,256,256]{3,1,0,2:T(1,128)} %collective-permute-done.1, f32[256,256]{1,0:T(8,128)S(1)} %bitcast.32, f32[5]{0:T(128)S(1)} %get-tuple-element.31, f32[5]{0:T(128)S(1)} %get-tuple-element.32, ...), kind=kLoop, calls=%fused_computation.4 | loop fusion | flops 8847360 | bytes 5505204 | tf_op jit(solution)/shard_map/add | solution.py:85
  39.0 1.9 %collective-permute-start.3 = (f32[5,1,256,256]{3,1,0,2:T(1,128)S(1)}, f32[5,1,256,256]{3,1,0,2:T(1,128)S(1)}, u32[]{:S(2)}, u32[]{:S(2)}) collective-permute-start(f32[5,1,256,256]{3,1,0,2:T(1,128)S(1)} %fusion), channel_id=1, source_target_pairs={{1,0},{2,1},{3,2},{4,3},{5,4},{6,5},{7,6},{8,7},{9,8},{10,9},{11,1... | collective-permute-start | bytes 3932168 | tf_op jit(solution)/shard_map/ppermute | solution.py:21
  41.0 3.6 %collective-permute-start.2 = (f32[5,1,256,256]{3,1,0,2:T(1,128)S(1)}, f32[5,1,256,256]{3,1,0,2:T(1,128)}, u32[]{:S(2)}, u32[]{:S(2)}) collective-permute-start(f32[5,1,256,256]{3,1,0,2:T(1,128)S(1)} %fusion), channel_id=1, source_target_pairs={{0,1},{1,2},{2,3},{3,4},{4,5},{5,6},{6,7},{7,8},{8,9},{9,10},{10,1... | collective-permute-start | bytes 3932168 | tf_op jit(solution)/shard_map/ppermute | solution.py:20
  44.6 13.3 %collective-permute-done.3 = f32[5,1,256,256]{3,1,0,2:T(1,128)S(1)} collective-permute-done((f32[5,1,256,256]{3,1,0,2:T(1,128)S(1)}, f32[5,1,256,256]{3,1,0,2:T(1,128)S(1)}, u32[]{:S(2)}, u32[]{:S(2)}) %collective-permute-start.3) | collective-permute-done | bytes 1310752 | tf_op jit(solution)/shard_map/ppermute | solution.py:21
  58.0 0.0 copy-start.1
  58.0 1.1 copy-done.1
  59.0 0.1 collective-permute-done.2
  59.2 12.0 %fusion.1 = f32[5,1,256,256]{3,1,0,2:T(1,128)S(1)} fusion(f32[5,1,256,256]{3,1,0,2:T(1,128)S(1)} %fusion, f32[5,1,256,256]{3,1,0,2:T(1,128)} %collective-permute-done.2, f32[5,1,256,256]{3,1,0,2:T(1,128)} %copy-done.1, f32[256,256]{1,0:T(8,128)S(1)} %bitcast.33, f32[5]{0:T(128)S(1)} %get-tuple-element.31, f32[5]{0:T(128)S(1)} %get-tuple-element.32, ...), kind=kLoop, calls=%fused_computation.5 | loop fusion | flops 8847360 | bytes 5505204 | tf_op jit(solution)/shard_map/add | solution.py:85
  71.2 0.5 constant_dynamic-slice_fusion
  71.6 7.0 %collective-permute-start.4 = (f32[5,1,128,256]{3,1,0,2:T(1,128)S(1)}, f32[5,1,128,256]{3,1,0,2:T(1,128)S(1)}, u32[]{:S(2)}, u32[]{:S(2)}) collective-permute-start(f32[5,1,128,256]{3,1,0,2:T(1,128)S(1)} %constant_dynamic-slice_fusion), channel_id=1, source_target_pairs={{0,128},{128,0},{1,129},{129,1},{2,130},{130,2},{3,131},{131,3},{4... | collective-permute-start | bytes 1966088 | tf_op jit(solution)/shard_map/ppermute | solution.py:33
  78.6 8.1 %collective-permute-done.4 = f32[5,1,128,256]{3,1,0,2:T(1,128)S(1)} collective-permute-done((f32[5,1,128,256]{3,1,0,2:T(1,128)S(1)}, f32[5,1,128,256]{3,1,0,2:T(1,128)S(1)}, u32[]{:S(2)}, u32[]{:S(2)}) %collective-permute-start.4) | collective-permute-done | bytes 655392 | tf_op jit(solution)/shard_map/ppermute | solution.py:33
  86.7 0.9 broadcast_select_fusion.1
  87.6 2.2 %pad_maximum_fusion.2 = f32[10,1,128,256]{3,1,0,2:T(1,128)} fusion(f32[5,1,128,256]{3,1,0,2:T(1,128)S(1)} %get-tuple-element.25, f32[5,1,128,256]{3,1,0,2:T(1,128)S(1)} %get-tuple-element.24), kind=kLoop, calls=%fused_computation.6 | loop fusion | flops 327680 | bytes 2621440 | tf_op jit(solution)/shard_map/concatenate | solution.py:135
  89.8 32.4 %all-to-all-start = ((f32[10,1,128,256]{3,1,0,2:T(1,128)}), f32[10,1,128,256]{3,1,0,2:T(1,128)S(1)}, u32[]{:S(2)}, u32[]{:S(2)}) async-start(f32[10,1,128,256]{3,1,0,2:T(1,128)} %pad_maximum_fusion.2), calls=%async_computation | async-start | bytes 2621440 | tf_op jit(solution)/shard_map/all_to_all | solution.py:136
  122.2 3.0 %fusion.2 = (f32[8,128,1,256]{3,2,1,0:T(1,128)S(1)}, f32[8,128,1,256]{3,2,1,0:T(1,128)S(1)}) fusion(f32[16,128,1,256]{3,2,1,0:T(1,128)} %param.15), kind=kLoop, calls=%fused_computation.39 | loop fusion | bytes 4194304 | tf_op jit(solution)/shard_map/slice | solution.py:111
  125.2 32.2 %all-to-all-done = f32[10,1,128,256]{3,1,0,2:T(1,128)S(1)} async-done(((f32[10,1,128,256]{3,1,0,2:T(1,128)}), f32[10,1,128,256]{3,1,0,2:T(1,128)S(1)}, u32[]{:S(2)}, u32[]{:S(2)}) %all-to-all-start) | async-done | bytes 1310752 | tf_op jit(solution)/shard_map/all_to_all | solution.py:136
  157.4 2.2 %copy_add_fusion = (f32[10,128,1,256]{3,1,0,2:T(8,128)S(1)}, f32[10,128,1,256]{3,1,0,2:T(8,128)S(1)}, f32[10,128,1,256]{3,1,0,2:T(8,128)S(1)}, f32[10,128,1,256]{3,1,0,2:T(8,128)S(1)}) fusion(f32[10,128,1,256]{3,2,1,0:T(1,128)} %param.14, f32[10,1,128,256]{3,1,0,2:T(1,128)S(1)} %all-to-all-done, f32[10,128,1,256]{3,2,1,0:T(1,128)} %param.13), kind=kLoop, calls=%fused_computation.9 | loop fusion | flops 1966080 | bytes 9175040 | tf_op jit(solution)/shard_map/add | solution.py:109
  159.6 2.4 %copy.62 = f32[10,128,1,256]{3,2,1,0:T(1,128)} copy(f32[10,128,1,256]{3,1,0,2:T(8,128)S(1)} %get-tuple-element.16) | data formatting | bytes 2621440
  162.1 0.5 rsqrt_multiply_fusion
  162.6 0.2 pad_maximum_fusion.1
  162.8 3.5 %copy.64 = f32[16,128,1,256]{3,2,1,0:T(1,128)} copy(f32[16,128,1,256]{3,1,0,2:T(8,128)S(1)} %pad_maximum_fusion.1) | data formatting | bytes 4194304
  166.3 2.4 %copy.61 = f32[10,128,1,256]{3,2,1,0:T(1,128)} copy(f32[10,128,1,256]{3,1,0,2:T(8,128)S(1)} %get-tuple-element.18) | data formatting | bytes 2621440
  168.7 0.2 pad_maximum_fusion
  168.9 3.5 %copy.63 = f32[16,128,1,256]{3,2,1,0:T(1,128)} copy(f32[16,128,1,256]{3,1,0,2:T(8,128)S(1)} %pad_maximum_fusion) | data formatting | bytes 4194304
  (6 shorter events, 0.1 us)
Async XLA Ops:
  0.6 9.4 %copy-start.5 = (f32[8]{0:T(128)S(1)}, f32[8]{0:T(128)}, u32[]{:S(2)}) copy-start(f32[8]{0:T(128)} %constant.45) | copy-start | bytes 100
  0.6 9.3 %copy-start.6 = (f32[8]{0:T(128)S(1)}, f32[8]{0:T(128)}, u32[]{:S(2)}) copy-start(f32[8]{0:T(128)} %constant.34.clone) | copy-start | bytes 100
  0.7 9.3 %copy-start.4 = (f32[8]{0:T(128)S(1)}, f32[8]{0:T(128)}, u32[]{:S(2)}) copy-start(f32[8]{0:T(128)} %param.12) | copy-start | bytes 100
  0.7 9.3 %copy-start.3 = (f32[8]{0:T(128)S(1)}, f32[8]{0:T(128)}, u32[]{:S(2)}) copy-start(f32[8]{0:T(128)} %param.11) | copy-start | bytes 100
  0.7 26.4 %copy-start.2 = (f32[1,256,256]{2,1,0:T(8,128)S(1)}, f32[1,256,256]{2,1,0:T(8,128)}, u32[]{:S(2)}) copy-start(f32[1,256,256]{2,1,0:T(8,128)} %param.10) | copy-start | bytes 786436
  3.4 19.1 %collective-permute-start = (f32[5,1,256,256]{3,1,0,2:T(1,128)S(1)}, f32[5,1,256,256]{3,1,0,2:T(1,128)S(1)}, u32[]{:S(2)}, u32[]{:S(2)}) collective-permute-start(f32[5,1,256,256]{3,1,0,2:T(1,128)S(1)} %copy.54), channel_id=1, source_target_pairs={{0,1},{1,2},{2,3},{3,4},{4,5},{5,6},{6,7},{7,8},{8,9},{9,10},{10,1... | collective-permute-start | bytes 3932168 | tf_op jit(solution)/shard_map/ppermute | solution.py:20
  8.0 19.0 %collective-permute-start.1 = (f32[5,1,256,256]{3,1,0,2:T(1,128)S(1)}, f32[5,1,256,256]{3,1,0,2:T(1,128)}, u32[]{:S(2)}, u32[]{:S(2)}) collective-permute-start(f32[5,1,256,256]{3,1,0,2:T(1,128)S(1)} %copy.54), channel_id=1, source_target_pairs={{1,0},{2,1},{3,2},{4,3},{5,4},{6,5},{7,6},{8,7},{9,8},{10,9},{11,1... | collective-permute-start | bytes 3932168 | tf_op jit(solution)/shard_map/ppermute | solution.py:21
  22.5 4.5 %copy-start = (f32[5,1,256,256]{3,1,0,2:T(1,128)}, f32[5,1,256,256]{3,1,0,2:T(1,128)S(1)}, u32[]{:S(2)}) copy-start(f32[5,1,256,256]{3,1,0,2:T(1,128)S(1)} %collective-permute-done) | copy-start | bytes 3932164
  39.0 18.9 %collective-permute-start.3 = (f32[5,1,256,256]{3,1,0,2:T(1,128)S(1)}, f32[5,1,256,256]{3,1,0,2:T(1,128)S(1)}, u32[]{:S(2)}, u32[]{:S(2)}) collective-permute-start(f32[5,1,256,256]{3,1,0,2:T(1,128)S(1)} %fusion), channel_id=1, source_target_pairs={{1,0},{2,1},{3,2},{4,3},{5,4},{6,5},{7,6},{8,7},{9,8},{10,9},{11,1... | collective-permute-start | bytes 3932168 | tf_op jit(solution)/shard_map/ppermute | solution.py:21
  41.0 18.2 %collective-permute-start.2 = (f32[5,1,256,256]{3,1,0,2:T(1,128)S(1)}, f32[5,1,256,256]{3,1,0,2:T(1,128)}, u32[]{:S(2)}, u32[]{:S(2)}) collective-permute-start(f32[5,1,256,256]{3,1,0,2:T(1,128)S(1)} %fusion), channel_id=1, source_target_pairs={{0,1},{1,2},{2,3},{3,4},{4,5},{5,6},{6,7},{7,8},{8,9},{9,10},{10,1... | collective-permute-start | bytes 3932168 | tf_op jit(solution)/shard_map/ppermute | solution.py:20
  58.0 1.1 copy-start.1
  71.6 15.1 %collective-permute-start.4 = (f32[5,1,128,256]{3,1,0,2:T(1,128)S(1)}, f32[5,1,128,256]{3,1,0,2:T(1,128)S(1)}, u32[]{:S(2)}, u32[]{:S(2)}) collective-permute-start(f32[5,1,128,256]{3,1,0,2:T(1,128)S(1)} %constant_dynamic-slice_fusion), channel_id=1, source_target_pairs={{0,128},{128,0},{1,129},{129,1},{2,130},{130,2},{3,131},{131,3},{4... | collective-permute-start | bytes 1966088 | tf_op jit(solution)/shard_map/ppermute | solution.py:33
  89.8 67.6 %all-to-all-start = ((f32[10,1,128,256]{3,1,0,2:T(1,128)}), f32[10,1,128,256]{3,1,0,2:T(1,128)S(1)}, u32[]{:S(2)}, u32[]{:S(2)}) async-start(f32[10,1,128,256]{3,1,0,2:T(1,128)} %pad_maximum_fusion.2), calls=%async_computation | async-start | bytes 2621440 | tf_op jit(solution)/shard_map/all_to_all | solution.py:136
where the time goes:
time: 173 us; the launch traced here: 172 us
  waiting for transfers between devices  70.7 us (41%)
  starting transfers between devices  51.5 us (30%)
  other arithmetic  30.3 us (18%)
  local copies, waits for them, and re-layouts  19 us (11%)
    all_to_all x1, starting transfers between devices, body(): lax.all_to_all(mine, 'brick', split_axis=2, concat_axis=1, tiled=True)  32.4 us
    all_to_all x1, waiting for transfers between devices, body(): lax.all_to_all(mine, 'brick', split_axis=2, concat_axis=1, tiled=True)  32.2 us
    add x2, other arithmetic, stencil_update(): return current + change  24 us
    ppermute x2, waiting for transfers between devices, with_halo(): after = lax.ppermute(initial, axis, down)  17.8 us
    unnamed x19, local copies, waits for them, and re-layouts  15.6 us
    ppermute x2, waiting for transfers between devices, with_halo(): before = lax.ppermute(last, axis, up)  12.5 us
    ppermute x2, starting transfers between devices, with_halo(): before = lax.ppermute(last, axis, up)  8.24 us
    ppermute x1, waiting for transfers between devices, swapped(): return lax.ppermute(block, axis, route)  8.12 us
  transfers between devices with their start and end apart: 6, of which 6 were waited for; matrix products, arithmetic and copies ran while one was open for 2% of the time, Pallas kernels for 0%

commit v1 on v0

v1 whole, which is shorter than its diff:
```python
import functools

import jax
import jax.numpy as jnp
import numpy as np
from jax import lax
from jax.experimental import pallas as pl
from jax.experimental.pallas import tpu as pltpu
from jax.sharding import PartitionSpec as P

PRIOR = 3
LOWER = np.asarray((0.02, 0.02, 0.02, 0.01, 0.0, 0.0, 0.5, 0.0), np.float32)
UPPER = np.asarray((0.12, 0.12, 0.12, 0.06, 0.2, 1.0, 1.5, 0.1), np.float32)
WIDTH = UPPER - LOWER
ROWS = 64
CHUNKS = (3, 2)


def physical_of(member, a_ref, b_ref):
    values = []
    for k in range(8):
        from_b = (member == 1) | (member == k + 2)
        unit = jnp.where(from_b, b_ref[k], a_ref[k])
        values.append(float(LOWER[k]) + float(WIDTH[k]) * unit)
    return values


def stencil_kernel(firsts, counts, strided, place_ref, a_ref, b_ref, source_ref, *refs):
    parts, outs = refs[: 3 * len(counts)], refs[3 * len(counts) :]
    side, core = place_ref[0], place_ref[1]
    ny, nz = source_ref.shape
    column = lax.broadcasted_iota(jnp.int32, (ROWS, nz), 1)
    zero = jnp.zeros((8, nz), jnp.float32)
    pieces = nz // 128
    pitch = sum(counts) * pieces
    done = 0
    for i, (first, count) in enumerate(zip(firsts, counts)):
        c_ref, near_ref, far_ref = parts[3 * i : 3 * i + 3]
        out_ref = outs[0] if strided else outs[i]

        def one_member(m, carry, c_ref=c_ref, near_ref=near_ref, far_ref=far_ref, out_ref=out_ref, first=first, done=done):
            drift_1, drift_2, drift_3, diffusion, decay, amplitude, anisotropy, reaction = physical_of(
                side * 5 + first + m, a_ref, b_ref
            )
            along = diffusion * anisotropy
            before = drift_1 + diffusion
            near_w = jnp.where(core == 0, diffusion, before)
            far_w = jnp.where(core == 0, before, diffusion)
            own_w = 1.0 - drift_1 - drift_2 - drift_3 - decay - diffusion * (4.0 + 2.0 * anisotropy)
            for r in range(0, ny, ROWS):
                c = c_ref[m, r : r + ROWS, :]
                above = c_ref[m, r - 8 : r, :] if r > 0 else zero
                below = c_ref[m, r + ROWS : r + ROWS + 8, :] if r + ROWS < ny else zero
                wide = jnp.concatenate([above, c, below], axis=0)
                y_before = pltpu.roll(wide, 1, 0)[8 : 8 + ROWS]
                y_after = pltpu.roll(wide, ROWS + 15, 0)[8 : 8 + ROWS]
                z_before = jnp.where(column == 0, 0.0, pltpu.roll(c, 1, 1))
                z_after = jnp.where(column == nz - 1, 0.0, pltpu.roll(c, nz - 1, 1))
                new = (
                    c * (own_w - reaction * jnp.abs(c))
                    + near_w * near_ref[m, r : r + ROWS, :]
                    + far_w * far_ref[m, r : r + ROWS, :]
                    + (drift_2 + diffusion) * y_before
                    + diffusion * y_after
                    + (drift_3 + along) * z_before
                    + along * z_after
                    + amplitude * source_ref[r : r + ROWS, :]
                )
                if strided:
                    for h in range(pieces):
                        start = r * pitch + (done + m) * pieces + h
                        out_ref[pl.ds(start, ROWS, stride=pitch), :] = new[:, h * 128 : (h + 1) * 128]
                else:
                    out_ref[m, r : r + ROWS, :] = new
            return carry

        lax.fori_loop(0, count, one_member, 0)
        done += count


def advance(place, params_a, params_b, source, parts, firsts, strided):
    counts = [own.shape[0] for own, _, _ in parts]
    ny, nz = source.shape
    whole = pl.BlockSpec(memory_space=pltpu.VMEM)
    scalars = pl.BlockSpec(memory_space=pltpu.SMEM)
    cells = sum(counts) * ny * nz
    if strided:
        out_shape = [jax.ShapeDtypeStruct((cells // 128, 128), jnp.float32)]
    else:
        out_shape = [jax.ShapeDtypeStruct(own.shape, jnp.float32) for own, _, _ in parts]
    return pl.pallas_call(
        functools.partial(stencil_kernel, firsts, counts, strided),
        in_specs=[scalars] * 3 + [whole] * (1 + 3 * len(parts)),
        out_specs=[whole] * len(out_shape),
        out_shape=out_shape,
        compiler_params=pltpu.CompilerParams(vmem_limit_bytes=32 * 1024 * 1024),
        cost_estimate=pl.CostEstimate(flops=20 * cells, bytes_accessed=16 * cells, transcendentals=0),
        name="advance_strips" if strided else "advance_planes",
    )(place, params_a, params_b, source, *[x for part in parts for x in part])


def accumulate_kernel(counts, xb, *refs):
    n = len(counts)
    gathered = refs[:n]
    means_ref, squares_ref, cross_ref = refs[n : n + 3]
    new_means_ref, new_squares_ref, new_cross_ref, maps_ref = refs[n + 3 : n + 7]
    held = refs[n + 7]
    members = 10
    first = 0
    for g, count in zip(gathered, counts):
        for s in range(2):
            for mm in range(count):
                for h in range(2):
                    held[s * 5 + first + mm, pl.ds(h, xb, stride=2), :] = g[
                        s, pl.ds(mm * 2 + h, xb, stride=2 * count), :
                    ]
        first += count
    base = []
    for m in (0, 1):
        out, mean = held[m], means_ref[m]
        deviation = out - mean
        new_mean = mean + deviation / float(PRIOR + 1)
        after = out - new_mean
        new_square = squares_ref[m] + deviation * after
        new_means_ref[m] = new_mean
        new_squares_ref[m] = new_square
        base.append((deviation, new_square))
    for m in range(2, members):
        k = m - 2
        out, mean = held[m], means_ref[m]
        deviation = out - mean
        new_mean = mean + deviation / float(PRIOR + 1)
        after = out - new_mean
        new_square = squares_ref[m] + deviation * after
        new_means_ref[m] = new_mean
        new_squares_ref[m] = new_square
        first_cross = cross_ref[k] + base[1][0] * after
        total_cross = cross_ref[8 + k] + base[0][0] * after
        new_cross_ref[k] = first_cross
        new_cross_ref[8 + k] = total_cross
        maps_ref[k] = first_cross * lax.rsqrt(base[1][1] * new_square)
        maps_ref[8 + k] = 1.0 - total_cross * lax.rsqrt(base[0][1] * new_square)


def accumulate(gathered, counts, means, squares, cross):
    xb = 32
    nx = 128
    block = lambda lead: pl.BlockSpec((lead, 2 * xb, 128), lambda i: (0, i, 0))
    shape = lambda lead: jax.ShapeDtypeStruct((lead, 2 * nx, 128), jnp.float32)
    return pl.pallas_call(
        functools.partial(accumulate_kernel, counts, xb),
        grid=(nx // xb,),
        in_specs=[pl.BlockSpec((2, xb * 2 * count, 128), lambda i: (0, i, 0)) for count in counts]
        + [block(10), block(10), block(16)],
        out_specs=[block(10), block(10), block(16), block(16)],
        out_shape=[shape(10), shape(10), shape(16), shape(16)],
        scratch_shapes=[pltpu.VMEM((10, 2 * xb, 128), jnp.float32)],
        compiler_params=pltpu.CompilerParams(vmem_limit_bytes=32 * 1024 * 1024),
        cost_estimate=pl.CostEstimate(
            flops=40 * 10 * nx * 256, bytes_accessed=13 * 1024 * 1024, transcendentals=16 * nx * 256
        ),
        name="accumulate",
    )(*gathered, means, squares, cross)


def routes(count):
    near = [(i, i ^ 1) for i in range(count)]
    far = [(i, i + 1) for i in range(1, count - 1, 2)]
    far += [(j, i) for i, j in far]
    return near, far


def body(fields, source_field, params_a, params_b, running_means, running_squares, running_cross):
    near_route, far_route = routes(lax.axis_size("brick"))
    place = jnp.stack([lax.axis_index("side"), lax.axis_index("brick") % 2]).astype(jnp.int32)
    fields = fields[:, 0]
    source = source_field[0]
    firsts = [sum(CHUNKS[:i]) for i in range(len(CHUNKS))]
    currents = [fields[f : f + n] for f, n in zip(firsts, CHUNKS)]
    halo = lambda c: (c, lax.ppermute(c, "brick", near_route), lax.ppermute(c, "brick", far_route))
    step = lambda parts, fs, last: advance(place, params_a, params_b, source, parts, fs, last)
    parts = [halo(c) for c in currents]
    currents = [step([part], [f], False)[0] for part, f in zip(parts, firsts)]
    (mine,) = step([halo(c) for c in currents], firsts, True)
    strips = lax.all_to_all(
        mine.reshape(256, 1, 5 * 256), ("side", "brick"), split_axis=0, concat_axis=0, tiled=True
    )
    gathered = [strips.reshape(2, 128 * 2 * 5, 128)]
    flat = lambda x: x.reshape(x.shape[0], 256, 128)
    outs = accumulate(
        gathered, (5,), flat(running_means), flat(running_squares), flat(running_cross)
    )
    return tuple(o.reshape(o.shape[0], 128, 1, 256) for o in outs)


def solution(mesh):
    strips = P(None, None, ("side", "brick"), None)
    return jax.shard_map(
        body,
        mesh=mesh,
        in_specs=(
            P("side", "brick", None, None),
            P("brick", None, None),
            P(),
            P(),
            strips,
            strips,
            strips,
        ),
        out_specs=(strips, strips, strips, strips),
        check_vma=False,
    )
```

time: 173 us -> 100 us (0.58)
  blocking collectives: 0 us -> 58 us
  waiting for transfers between devices: 70.7 us -> 14.4 us
  starting transfers between devices: 51.5 us -> 15.8 us
  other arithmetic: 30.3 us -> 0.08 us
  local copies, waits for them, and re-layouts: 19 us -> 2.34 us
  Pallas kernels: 0 us -> 8.48 us
    all_to_all x0 -> x1, blocking collectives: none -> 58 us  [body(): lax.all_to_all(mine.reshape(256, 1, 5 * 256), ('side', 'brick'), split_ax...]
    all_to_all x1 -> x0, starting transfers between devices: 32.4 us -> none  [body(): lax.all_to_all(mine, 'brick', split_axis=2, concat_axis=1, tiled=True)]
    all_to_all x1 -> x0, waiting for transfers between devices: 32.2 us -> none  [body(): lax.all_to_all(mine, 'brick', split_axis=2, concat_axis=1, tiled=True)]
    add x7 -> x0, other arithmetic: 26.3 us -> none  [the longest x2 24 us: stencil_update(): return current + change]
    ppermute x5 -> x8, waiting for transfers between devices: 38.5 us -> 14.4 us  [the longest x4 14.4 us: body(): lax.ppermute(c, 'brick', far_route)]
    unnamed x19 -> x12, local copies, waits for them, and re-layouts: 15.6 us -> 0.03 us
    pallas_call x0 -> x4, Pallas kernels: none -> 8.48 us  [the longest x3 4.8 us: advance(): pl.pallas_call(functools.partial(stencil_kernel, firsts, counts, strided)...]
    ppermute x5 -> x8, starting transfers between devices: 19.1 us -> 15.8 us  [the longest x4 15.5 us: body(): lax.ppermute(c, 'brick', far_route)]
  transfers between devices with their start and end apart: 6 -> 8, of which waited for: 6 -> 3; matrix products, arithmetic and copies ran while one was open for 2% -> 1% of each run, Pallas kernels for 0% -> 3%
where the time goes in v1:
time: 100 us
  blocking collectives  58 us (58%)
  starting transfers between devices  15.8 us (16%)
  waiting for transfers between devices  14.4 us (14%)
  Pallas kernels  8.48 us (8%)
  local copies, waits for them, and re-layouts  2.34 us (2%)
    all_to_all x1, blocking collectives, body(): lax.all_to_all(mine.reshape(256, 1, 5 * 256), ('side', 'brick'), split_ax...  58 us
    ppermute x4, starting transfers between devices, body(): lax.ppermute(c, 'brick', far_route)  15.5 us
    ppermute x4, waiting for transfers between devices, body(): lax.ppermute(c, 'brick', far_route)  14.4 us
    pallas_call x3, Pallas kernels, advance(): pl.pallas_call(functools.partial(stencil_kernel, firsts, counts, strided)...  4.8 us
    pallas_call x1, Pallas kernels, accumulate(): pl.pallas_call(functools.partial(accumulate_kernel, counts, xb), grid=(nx...  3.68 us
    slice x2, local copies, waits for them, and re-layouts, body(): currents = [fields[f:f + n] for f, n in zip(firsts, CHUNKS)]  2.3 us
  transfers between devices with their start and end apart: 8, of which 3 were waited for; matrix products, arithmetic and copies ran while one was open for 1% of the time, Pallas kernels for 3%

profile of v1, /device:TPU:1, one launch (start us, length us, event | category | flops | bytes accessed | tf_op | source)
XLA Modules:
  0.0 100.0 jit_solution(12790967449348422938)
XLA Ops:
  0.6 0.0 copy-start
  0.6 0.0 copy-start.4
  0.7 0.0 copy-start.5
  0.7 1.2 %slice_bitcast_fusion.refs_0_ = f32[3,256,256]{2,1,0:T(8,128)S(1)} fusion(f32[5,1,256,256]{3,2,0,1:T(8,128)} %bitcast.25), kind=kLoop, calls=%fused_computation | loop fusion | bytes 1572864 | tf_op jit(solution)/shard_map/slice | solution.py:179
  1.9 4.6 %collective-permute-start.1 = (f32[3,256,256]{2,1,0:T(8,128)S(1)}, f32[3,256,256]{2,1,0:T(8,128)S(1)}, u32[]{:S(2)}, u32[]{:S(2)}) collective-permute-start(f32[3,256,256]{2,1,0:T(8,128)S(1)} %slice_bitcast_fusion.refs_0_), channel_id=1, source_target_pairs={{1,2},{3,4},{5,6},{7,8},{9,10},{11,12},{13,14},{15,16},{17,18},{19... | collective-permute-start | bytes 2359304 | tf_op jit(solution)/shard_map/ppermute | solution.py:180
  6.5 0.1 collective-permute-start
  6.6 1.1 %slice_bitcast_fusion.1.refs_0_ = f32[2,256,256]{2,1,0:T(8,128)S(1)} fusion(f32[5,1,256,256]{3,2,0,1:T(8,128)} %bitcast.26), kind=kLoop, calls=%fused_computation.1 | loop fusion | bytes 1048576 | tf_op jit(solution)/shard_map/slice | solution.py:179
  7.7 3.6 %collective-permute-start.5 = (f32[2,256,256]{2,1,0:T(8,128)S(1)}, f32[2,256,256]{2,1,0:T(8,128)}, u32[]{:S(2)}, u32[]{:S(2)}) collective-permute-start(f32[2,256,256]{2,1,0:T(8,128)S(1)} %slice_bitcast_fusion.1.refs_0_), channel_id=1, source_target_pairs={{1,2},{3,4},{5,6},{7,8},{9,10},{11,12},{13,14},{15,16},{17,18},{19... | collective-permute-start | bytes 1572872 | tf_op jit(solution)/shard_map/ppermute | solution.py:180
  11.3 0.1 collective-permute-start.4
  11.4 0.1 pad_add_fusion.place_ref
  11.5 4.7 %collective-permute-done.1.refs_2_ = f32[3,256,256]{2,1,0:T(8,128)S(1)} collective-permute-done((f32[3,256,256]{2,1,0:T(8,128)S(1)}, f32[3,256,256]{2,1,0:T(8,128)S(1)}, u32[]{:S(2)}, u32[]{:S(2)}) %collective-permute-start.1) | collective-permute-done | bytes 786464 | tf_op jit(solution)/shard_map/ppermute | solution.py:180
  16.2 0.0 collective-permute-done.refs_1_
  16.2 0.0 copy-done
  16.2 0.0 copy-done.4
  16.2 0.0 copy-done.5
  16.2 1.3 %advance_planes.2.refs_0_ = f32[3,256,256]{2,1,0:T(8,128)S(1)} custom-call(s32[2]{0:T(128)S(1)} %pad_add_fusion.place_ref, f32[8]{0:T(128)S(1)} %copy-done.4, f32[8]{0:T(128)S(1)} %copy-done.5, f32[256,256]{1,0:T(8,128)S(1)} %bitcast.19, f32[3,256,256]{2,1,0:T(8,128)S(1)} %slice_bitcast_fusion.refs_0_, f32[3,256,256]{2,1,0:T(8,128)S(1)} %collective-permute-done.refs_1_, ...), custom_call_target="tpu_custom_call" | custom-call | flops 3932160 | bytes 3145728 | tf_op jit(solution)/shard_map/advance_planes/pallas_call | solution.py:91
  17.5 3.6 %collective-permute-start.3 = (f32[3,256,256]{2,1,0:T(8,128)S(1)}, f32[3,256,256]{2,1,0:T(8,128)S(1)}, u32[]{:S(2)}, u32[]{:S(2)}) collective-permute-start(f32[3,256,256]{2,1,0:T(8,128)S(1)} %advance_planes.2.refs_0_), channel_id=1, source_target_pairs={{1,2},{3,4},{5,6},{7,8},{9,10},{11,12},{13,14},{15,16},{17,18},{19... | collective-permute-start | bytes 2359304 | tf_op jit(solution)/shard_map/ppermute | solution.py:180
  21.1 0.1 collective-permute-start.2
  21.2 0.7 collective-permute-done.5.refs_2_
  21.9 0.0 collective-permute-done.4.refs_1_
  21.9 1.7 %advance_planes.3.refs_3_ = f32[2,256,256]{2,1,0:T(8,128)S(1)} custom-call(s32[2]{0:T(128)S(1)} %pad_add_fusion.place_ref, f32[8]{0:T(128)S(1)} %copy-done.4, f32[8]{0:T(128)S(1)} %copy-done.5, f32[256,256]{1,0:T(8,128)S(1)} %bitcast.20, f32[2,256,256]{2,1,0:T(8,128)S(1)} %slice_bitcast_fusion.1.refs_0_, f32[2,256,256]{2,1,0:T(8,128)} %collective-permute-done.4.refs_1_, ...), custom_call_target="tpu_custom_call" | custom-call | flops 2621440 | bytes 2097152 | tf_op jit(solution)/shard_map/advance_planes/pallas_call | solution.py:91
  23.6 3.6 %collective-permute-start.7 = (f32[2,256,256]{2,1,0:T(8,128)S(1)}, f32[2,256,256]{2,1,0:T(8,128)S(1)}, u32[]{:S(2)}, u32[]{:S(2)}) collective-permute-start(f32[2,256,256]{2,1,0:T(8,128)S(1)} %advance_planes.3.refs_3_), channel_id=1, source_target_pairs={{1,2},{3,4},{5,6},{7,8},{9,10},{11,12},{13,14},{15,16},{17,18},{19... | collective-permute-start | bytes 1572872 | tf_op jit(solution)/shard_map/ppermute | solution.py:180
  27.2 0.1 collective-permute-start.6
  27.3 9.1 %collective-permute-done.7.refs_5_ = f32[2,256,256]{2,1,0:T(8,128)S(1)} collective-permute-done((f32[2,256,256]{2,1,0:T(8,128)S(1)}, f32[2,256,256]{2,1,0:T(8,128)S(1)}, u32[]{:S(2)}, u32[]{:S(2)}) %collective-permute-start.7) | collective-permute-done | bytes 524320 | tf_op jit(solution)/shard_map/ppermute | solution.py:180
  36.4 0.0 collective-permute-done.6.refs_4_
  36.4 0.0 collective-permute-done.3.refs_2_
  36.4 0.0 collective-permute-done.2.refs_1_
  36.4 0.0 copy-start.2
  36.4 0.0 copy-start.3
  36.4 1.8 %advance_strips.1 = f32[2560,128]{1,0:T(8,128)S(1)} custom-call(s32[2]{0:T(128)S(1)} %pad_add_fusion.place_ref, f32[8]{0:T(128)S(1)} %copy-done.4, f32[8]{0:T(128)S(1)} %copy-done.5, f32[256,256]{1,0:T(8,128)S(1)} %bitcast.21, f32[3,256,256]{2,1,0:T(8,128)S(1)} %advance_planes.2.refs_0_, f32[3,256,256]{2,1,0:T(8,128)S(1)} %collective-permute-done.2.refs_1_, ...), custom_call_target="tpu_custom_call" | custom-call | flops 6553600 | bytes 5242880 | tf_op jit(solution)/shard_map/advance_strips/pallas_call | solution.py:91
  38.3 0.0 copy-start.1
  38.3 58.0 %all_to_all.5 = f32[256,1,1280]{2,1,0:T(1,128)S(1)} all-to-all(f32[256,1,1280]{2,1,0:T(1,128)S(1)} %bitcast.17), channel_id=1, replica_groups=mesh['side'=2,'brick'=128] {'side','brick'}, dimensions={0} | all-to-all | bytes 2621440 | tf_op jit(solution)/shard_map/all_to_all | solution.py:185
  96.3 0.0 copy-done.2
  96.3 0.0 copy-done.3
  96.3 0.0 copy-done.1
  96.3 3.7 %accumulate.1 = (f32[10,256,128]{2,1,0:T(8,128)}, f32[10,256,128]{2,1,0:T(8,128)}, f32[16,256,128]{2,1,0:T(8,128)}, f32[16,256,128]{2,1,0:T(8,128)}) custom-call(f32[2,1280,128]{2,1,0:T(8,128)S(1)} %bitcast.18, f32[10,256,128]{2,1,0:T(8,128)S(1)} %bitcast.23, f32[10,256,128]{2,1,0:T(8,128)S(1)} %bitcast.24, f32[16,256,128]{2,1,0:T(8,128)S(1)} %bitcast.22), custom_call_target="tpu_custom_call" | custom-call | flops 13107200 | bytes 13631488 | tf_op jit(solution)/shard_map/accumulate/pallas_call | solution.py:150
Async XLA Ops:
  0.6 15.5 %copy-start = (f32[1,256,256]{2,1,0:T(8,128)S(1)}, f32[1,256,256]{2,1,0:T(8,128)}, u32[]{:S(2)}) copy-start(f32[1,256,256]{2,1,0:T(8,128)} %param.8) | copy-start | bytes 786436
  0.6 15.5 %copy-start.4 = (f32[8]{0:T(128)S(1)}, f32[8]{0:T(128)}, u32[]{:S(2)}) copy-start(f32[8]{0:T(128)} %a_ref.5) | copy-start | bytes 100
  0.7 15.5 %copy-start.5 = (f32[8]{0:T(128)S(1)}, f32[8]{0:T(128)}, u32[]{:S(2)}) copy-start(f32[8]{0:T(128)} %b_ref.5) | copy-start | bytes 100
  1.9 14.3 %collective-permute-start.1 = (f32[3,256,256]{2,1,0:T(8,128)S(1)}, f32[3,256,256]{2,1,0:T(8,128)S(1)}, u32[]{:S(2)}, u32[]{:S(2)}) collective-permute-start(f32[3,256,256]{2,1,0:T(8,128)S(1)} %slice_bitcast_fusion.refs_0_), channel_id=1, source_target_pairs={{1,2},{3,4},{5,6},{7,8},{9,10},{11,12},{13,14},{15,16},{17,18},{19... | collective-permute-start | bytes 2359304 | tf_op jit(solution)/shard_map/ppermute | solution.py:180
  6.5 9.7 %collective-permute-start = (f32[3,256,256]{2,1,0:T(8,128)S(1)}, f32[3,256,256]{2,1,0:T(8,128)S(1)}, u32[]{:S(2)}, u32[]{:S(2)}) collective-permute-start(f32[3,256,256]{2,1,0:T(8,128)S(1)} %slice_bitcast_fusion.refs_0_), channel_id=1, source_target_pairs={{0,1},{1,0},{2,3},{3,2},{4,5},{5,4},{6,7},{7,6},{8,9},{9,8},{10,11... | collective-permute-start | bytes 2359304 | tf_op jit(solution)/shard_map/ppermute | solution.py:180
  7.7 14.2 %collective-permute-start.5 = (f32[2,256,256]{2,1,0:T(8,128)S(1)}, f32[2,256,256]{2,1,0:T(8,128)}, u32[]{:S(2)}, u32[]{:S(2)}) collective-permute-start(f32[2,256,256]{2,1,0:T(8,128)S(1)} %slice_bitcast_fusion.1.refs_0_), channel_id=1, source_target_pairs={{1,2},{3,4},{5,6},{7,8},{9,10},{11,12},{13,14},{15,16},{17,18},{19... | collective-permute-start | bytes 1572872 | tf_op jit(solution)/shard_map/ppermute | solution.py:180
  11.3 10.6 %collective-permute-start.4 = (f32[2,256,256]{2,1,0:T(8,128)S(1)}, f32[2,256,256]{2,1,0:T(8,128)}, u32[]{:S(2)}, u32[]{:S(2)}) collective-permute-start(f32[2,256,256]{2,1,0:T(8,128)S(1)} %slice_bitcast_fusion.1.refs_0_), channel_id=1, source_target_pairs={{0,1},{1,0},{2,3},{3,2},{4,5},{5,4},{6,7},{7,6},{8,9},{9,8},{10,11... | collective-permute-start | bytes 1572872 | tf_op jit(solution)/shard_map/ppermute | solution.py:180
  17.5 18.9 %collective-permute-start.3 = (f32[3,256,256]{2,1,0:T(8,128)S(1)}, f32[3,256,256]{2,1,0:T(8,128)S(1)}, u32[]{:S(2)}, u32[]{:S(2)}) collective-permute-start(f32[3,256,256]{2,1,0:T(8,128)S(1)} %advance_planes.2.refs_0_), channel_id=1, source_target_pairs={{1,2},{3,4},{5,6},{7,8},{9,10},{11,12},{13,14},{15,16},{17,18},{19... | collective-permute-start | bytes 2359304 | tf_op jit(solution)/shard_map/ppermute | solution.py:180
  21.1 15.3 %collective-permute-start.2 = (f32[3,256,256]{2,1,0:T(8,128)S(1)}, f32[3,256,256]{2,1,0:T(8,128)S(1)}, u32[]{:S(2)}, u32[]{:S(2)}) collective-permute-start(f32[3,256,256]{2,1,0:T(8,128)S(1)} %advance_planes.2.refs_0_), channel_id=1, source_target_pairs={{0,1},{1,0},{2,3},{3,2},{4,5},{5,4},{6,7},{7,6},{8,9},{9,8},{10,11... | collective-permute-start | bytes 2359304 | tf_op jit(solution)/shard_map/ppermute | solution.py:180
  23.6 12.8 %collective-permute-start.7 = (f32[2,256,256]{2,1,0:T(8,128)S(1)}, f32[2,256,256]{2,1,0:T(8,128)S(1)}, u32[]{:S(2)}, u32[]{:S(2)}) collective-permute-start(f32[2,256,256]{2,1,0:T(8,128)S(1)} %advance_planes.3.refs_3_), channel_id=1, source_target_pairs={{1,2},{3,4},{5,6},{7,8},{9,10},{11,12},{13,14},{15,16},{17,18},{19... | collective-permute-start | bytes 1572872 | tf_op jit(solution)/shard_map/ppermute | solution.py:180
  27.2 9.2 %collective-permute-start.6 = (f32[2,256,256]{2,1,0:T(8,128)S(1)}, f32[2,256,256]{2,1,0:T(8,128)S(1)}, u32[]{:S(2)}, u32[]{:S(2)}) collective-permute-start(f32[2,256,256]{2,1,0:T(8,128)S(1)} %advance_planes.3.refs_3_), channel_id=1, source_target_pairs={{0,1},{1,0},{2,3},{3,2},{4,5},{5,4},{6,7},{7,6},{8,9},{9,8},{10,11... | collective-permute-start | bytes 1572872 | tf_op jit(solution)/shard_map/ppermute | solution.py:180
  36.4 59.9 %copy-start.2 = (f32[10,128,1,256]{3,2,1,0:T(1,128)S(1)}, f32[10,128,1,256]{3,2,1,0:T(1,128)}, u32[]{:S(2)}) copy-start(f32[10,128,1,256]{3,2,1,0:T(1,128)} %param.11) | copy-start | bytes 3932164
  36.4 59.9 %copy-start.3 = (f32[10,128,1,256]{3,2,1,0:T(1,128)S(1)}, f32[10,128,1,256]{3,2,1,0:T(1,128)}, u32[]{:S(2)}) copy-start(f32[10,128,1,256]{3,2,1,0:T(1,128)} %param.12) | copy-start | bytes 3932164
  38.3 58.0 %copy-start.1 = (f32[16,128,1,256]{3,2,1,0:T(1,128)S(1)}, f32[16,128,1,256]{3,2,1,0:T(1,128)}, u32[]{:S(2)}) copy-start(f32[16,128,1,256]{3,2,1,0:T(1,128)} %param.13) | copy-start | bytes 6291460

commit v2 on v1

v2 whole, which is shorter than its diff:
```python
import functools

import jax
import jax.numpy as jnp
import numpy as np
from jax import lax
from jax.experimental import pallas as pl
from jax.experimental.pallas import tpu as pltpu
from jax.sharding import PartitionSpec as P

PRIOR = 3
LOWER = np.asarray((0.02, 0.02, 0.02, 0.01, 0.0, 0.0, 0.5, 0.0), np.float32)
UPPER = np.asarray((0.12, 0.12, 0.12, 0.06, 0.2, 1.0, 1.5, 0.1), np.float32)
WIDTH = UPPER - LOWER
ROWS = 64


def weights_of(table_ref, m):
    member = table_ref[16] + jnp.asarray(m, jnp.float32)
    values = []
    for k in range(8):
        from_b = (member == 1.0) | (member == float(k + 2))
        unit = jnp.where(from_b, table_ref[8 + k], table_ref[k])
        values.append(float(LOWER[k]) + float(WIDTH[k]) * unit)
    drift_1, drift_2, drift_3, diffusion, decay, amplitude, anisotropy, reaction = values
    along = diffusion * anisotropy
    before = drift_1 + diffusion
    near_w = jnp.where(table_ref[17] == 0.0, diffusion, before)
    far_w = jnp.where(table_ref[17] == 0.0, before, diffusion)
    own_w = 1.0 - drift_1 - drift_2 - drift_3 - decay - diffusion * (4.0 + 2.0 * anisotropy)
    return own_w, near_w, far_w, drift_2 + diffusion, diffusion, drift_3 + along, along, amplitude, reaction


def step_plane(shape, weights, load, near, rest, store):
    own_w, near_w, _, y_before_w, y_after_w, z_before_w, z_after_w, _, reaction = weights
    ny, nz = shape
    column = lax.broadcasted_iota(jnp.int32, (ROWS, nz), 1)
    zero = jnp.zeros((8, nz), jnp.float32)
    for r in range(0, ny, ROWS):
        c = load(r, ROWS)
        above = load(r - 8, 8) if r > 0 else zero
        below = load(r + ROWS, 8) if r + ROWS < ny else zero
        wide = jnp.concatenate([above, c, below], axis=0)
        y_before = pltpu.roll(wide, 1, 0)[8 : 8 + ROWS]
        y_after = pltpu.roll(wide, ROWS + 15, 0)[8 : 8 + ROWS]
        z_before = jnp.where(column == 0, 0.0, pltpu.roll(c, 1, 1))
        z_after = jnp.where(column == nz - 1, 0.0, pltpu.roll(c, nz - 1, 1))
        new = (
            c * (own_w - reaction * jnp.abs(c))
            + near_w * near(r, ROWS)
            + y_before_w * y_before
            + y_after_w * y_after
            + z_before_w * z_before
            + z_after_w * z_after
            + rest(r, ROWS)
        )
        store(r, new)


def reader(ref, *at):
    return lambda r, n: ref[(*at, slice(r, r + n), slice(None))]


def store_strips(out_ref, m, count, r, new):
    pieces = new.shape[1] // 128
    pitch = count * pieces
    for h in range(pieces):
        start = r * pitch + m * pieces + h
        out_ref[pl.ds(start, new.shape[0], stride=pitch), :] = new[:, h * 128 : (h + 1) * 128]


def send_kernel(
    table_ref, raw_ref, source_ref, near_source_ref, near_ref, out_ref, partial_ref, copy_ref, source_copy_ref
):
    m = pl.program_id(0)
    weights = weights_of(table_ref, m)
    far_w, amplitude = weights[2], weights[7]
    count, ny, nz = copy_ref.shape
    for r in range(0, ny, ROWS):
        raw = raw_ref[0, r : r + ROWS, :]
        rest = far_w * raw + amplitude * near_source_ref[r : r + ROWS, :]
        store_strips(out_ref, m, count, r, far_w * rest)
        copy_ref[m, r : r + ROWS, :] = raw

    def store(r, new):
        partial_ref[m, r : r + ROWS, :] = new

    rest = lambda r, n: amplitude * source_ref[r : r + n, :]
    step_plane((ny, nz), weights, reader(raw_ref, 0), reader(near_ref, m), rest, store)

    @pl.when(m == 0)
    def _():
        for r in range(0, ny, ROWS):
            source_copy_ref[r : r + ROWS, :] = source_ref[r : r + ROWS, :]


def first_kernel(table_ref, partial_ref, far_ref, *out_refs):
    first = 0
    ny = far_ref.shape[1]
    for out_ref in out_refs:

        def one_member(j, carry, out_ref=out_ref, first=first):
            m = first + j
            far_w = weights_of(table_ref, m)[2]
            for r in range(0, ny, ROWS):
                rows = slice(r, r + ROWS)
                out_ref[j, rows, :] = partial_ref[m, rows, :] + far_w * far_ref[m, rows, :]
            return carry

        lax.fori_loop(0, out_ref.shape[0], one_member, 0)
        first += out_ref.shape[0]


def far_kernel(table_ref, raw_ref, raw_far_ref, out_ref):
    inside = table_ref[18] > 0.0

    def one_member(m, carry):
        weights = weights_of(table_ref, m)
        far_w = weights[2]

        def store(r, new):
            out_ref[m, r : r + ROWS, :] = jnp.where(inside, far_w * new, 0.0)

        step_plane(raw_ref.shape[1:], weights, reader(raw_far_ref, m), reader(raw_ref, m), lambda r, n: 0.0, store)
        return carry

    lax.fori_loop(0, raw_ref.shape[0], one_member, 0)


def second_kernel(table_ref, source_ref, far_part_ref, *refs):
    out_ref = refs[-1]
    count, ny, nz = far_part_ref.shape
    first = 0
    for own_ref, near_ref in zip(refs[:-1:2], refs[1:-1:2]):

        def one_member(j, carry, own_ref=own_ref, near_ref=near_ref, first=first):
            m = first + j
            weights = weights_of(table_ref, m)
            amplitude = weights[7]
            rest = lambda r, n: far_part_ref[m, r : r + n, :] + amplitude * source_ref[r : r + n, :]
            step_plane(
                (ny, nz), weights, reader(own_ref, j), reader(near_ref, j), rest,
                lambda r, new: store_strips(out_ref, m, count, r, new),
            )
            return carry

        lax.fori_loop(0, own_ref.shape[0], one_member, 0)
        first += own_ref.shape[0]


def add_kernel(table_ref, first_ref, second_ref, out_ref):
    rows = 160

    def some_rows(i, carry):
        at = pl.ds(pl.multiple_of(i * rows, rows), rows)
        out_ref[at, :] = first_ref[at, :] + second_ref[at, :]
        return carry

    lax.fori_loop(0, out_ref.shape[0] // rows, some_rows, 0)


def call(kernel, name, table, arrays, out_shapes, cells, scratch=(), grid=(), in_specs=None):
    whole = pl.BlockSpec(memory_space=pltpu.VMEM)
    return pl.pallas_call(
        kernel,
        grid=grid,
        in_specs=[pl.BlockSpec(memory_space=pltpu.SMEM)] + (in_specs or [whole] * len(arrays)),
        out_specs=[whole] * len(out_shapes),
        out_shape=[jax.ShapeDtypeStruct(shape, jnp.float32) for shape in out_shapes],
        scratch_shapes=scratch,
        compiler_params=pltpu.CompilerParams(vmem_limit_bytes=32 * 1024 * 1024),
        cost_estimate=pl.CostEstimate(flops=cells // 64, bytes_accessed=cells // 64, transcendentals=0),
        name=name,
    )(table, *arrays)


def accumulate_kernel(count, xb, gathered, means_ref, squares_ref, cross_ref, *outs):
    new_means_ref, new_squares_ref, new_cross_ref, maps_ref, held = outs
    i = pl.program_id(0)
    rows = pl.ds(pl.multiple_of(i * 2 * xb, 2 * xb), 2 * xb)
    for s in range(2):
        for m in range(count):
            for h in range(2):
                held[s * count + m, pl.ds(h, xb, stride=2), :] = gathered[
                    s, pl.ds(i * (xb * 2 * count) + m * 2 + h, xb, stride=2 * count), :
                ]

    def moments(m):
        out, mean = held[m], means_ref[m, rows, :]
        deviation = out - mean
        new_mean = mean + deviation * (1.0 / (PRIOR + 1))
        after = out - new_mean
        new_square = squares_ref[m, rows, :] + deviation * after
        new_means_ref[m] = new_mean
        new_squares_ref[m] = new_square
        return deviation, after, new_square

    base = [moments(0), moments(1)]
    for m in range(2, 2 * count):
        k = m - 2
        _, after, new_square = moments(m)
        first_cross = cross_ref[k, rows, :] + base[1][0] * after
        total_cross = cross_ref[8 + k, rows, :] + base[0][0] * after
        new_cross_ref[k] = first_cross
        new_cross_ref[8 + k] = total_cross
        maps_ref[k] = first_cross * lax.rsqrt(base[1][2] * new_square)
        maps_ref[8 + k] = 1.0 - total_cross * lax.rsqrt(base[0][2] * new_square)


def accumulate(gathered, count, means, squares, cross):
    xb = 32
    nx = 128
    whole = pl.BlockSpec(memory_space=pltpu.VMEM)
    block = lambda lead: pl.BlockSpec((lead, 2 * xb, 128), lambda i: (0, i, 0))
    shape = lambda lead: jax.ShapeDtypeStruct((lead, 2 * nx, 128), jnp.float32)
    return pl.pallas_call(
        functools.partial(accumulate_kernel, count, xb),
        grid=(nx // xb,),
        in_specs=[whole] * 4,
        out_specs=[block(10), block(10), block(16), block(16)],
        out_shape=[shape(10), shape(10), shape(16), shape(16)],
        scratch_shapes=[pltpu.VMEM((10, 2 * xb, 128), jnp.float32)],
        compiler_params=pltpu.CompilerParams(vmem_limit_bytes=32 * 1024 * 1024),
        cost_estimate=pl.CostEstimate(
            flops=40 * 10 * nx * 256, bytes_accessed=13 * 1024 * 1024, transcendentals=16 * nx * 256
        ),
        name="accumulate",
    )(gathered, means, squares, cross)


def routes(count):
    near = [(i, i ^ 1) for i in range(count)]
    far = [(i, i + 1) for i in range(1, count - 1, 2)]
    far += [(j, i) for i, j in far]
    second = [(i, i + 2) for i in range(0, count - 2, 2)] + [(i, i - 2) for i in range(3, count, 2)]
    return near, far, second


def body(fields, source_field, params_a, params_b, running_means, running_squares, running_cross):
    bricks = lax.axis_size("brick")
    near_route, far_route, second_route = routes(bricks)
    brick = lax.axis_index("brick")
    count = fields.shape[0]
    inside = (brick > 0) & (brick < bricks - 1)
    place = jnp.stack([lax.axis_index("side") * count, brick & 1, inside.astype(brick.dtype)])
    table = jnp.concatenate([params_a, params_b, place.astype(jnp.float32)])
    raw = fields[:, 0]
    source = source_field[0]
    send = lambda x, route: lax.ppermute(x, "brick", route)
    ny, nz = source.shape
    near_source = send(source, near_route)
    far = send(raw, far_route)
    near = send(raw, near_route)
    plane = lambda index: pl.BlockSpec((1, ny, nz), index)
    flat_shape = (raw.size // 128, 128)
    flat_plane = pl.BlockSpec((ny, nz), lambda m: (0, 0))
    beyond, partial, raw, source = call(
        send_kernel, "send_planes", table, (raw, source, near_source, near),
        (flat_shape, raw.shape, raw.shape, source.shape), raw.size, grid=(count,),
        in_specs=[plane(lambda m: (m, 0, 0)), flat_plane, flat_plane, pl.BlockSpec(memory_space=pltpu.VMEM)],
    )
    beyond = send(beyond, second_route)
    half = (count + 1) // 2
    ahead = call(
        first_kernel, "first_step", table, (partial, far), ((half, ny, nz), (count - half, ny, nz)), raw.size
    )
    pairs = [x for piece in ahead for x in (piece, send(piece, near_route))]
    (far_part,) = call(far_kernel, "far_step", table, (raw, far), (raw.shape,), raw.size)
    (mine,) = call(second_kernel, "second_step", table, (source, far_part, *pairs), (flat_shape,), raw.size)
    (mine,) = call(add_kernel, "add_beyond", table, (mine, beyond), (flat_shape,), raw.size // 8)
    strips = lax.all_to_all(
        mine.reshape(256, 1, count * 256), ("side", "brick"), split_axis=0, concat_axis=0, tiled=True
    )
    gathered = strips.reshape(2, 128 * 2 * count, 128)
    flat = lambda x: x.reshape(x.shape[0], 256, 128)
    outs = accumulate(
        gathered, count, flat(running_means), flat(running_squares), flat(running_cross)
    )
    return tuple(o.reshape(o.shape[0], 128, 1, 256) for o in outs)


def solution(mesh):
    strips = P(None, None, ("side", "brick"), None)
    return jax.shard_map(
        body,
        mesh=mesh,
        in_specs=(
            P("side", "brick", None, None),
            P("brick", None, None),
            P(),
            P(),
            strips,
            strips,
            strips,
        ),
        out_specs=(strips, strips, strips, strips),
        check_vma=False,
    )
```

time: 100 us -> 93.6 us (0.936)
  starting transfers between devices: 15.8 us -> 7.21 us
  blocking collectives: 58 us -> 52.2 us
  waiting for transfers between devices: 14.4 us -> 19.7 us
  Pallas kernels: 8.48 us -> 10.5 us
    ppermute x8 -> x6, starting transfers between devices: 15.8 us -> 7.21 us  [body(): send = lambda x, route: lax.ppermute(x, 'brick', route)]
    all_to_all x1, blocking collectives: 58 us -> 52.2 us  [body(): lax.all_to_all(mine.reshape(256, 1, count * 256), ('side', 'brick'), spli...]
    ppermute x8 -> x6, waiting for transfers between devices: 14.4 us -> 19.7 us  [body(): send = lambda x, route: lax.ppermute(x, 'brick', route)]
    slice x2 -> x0, local copies, waits for them, and re-layouts: 2.3 us -> none  [body(): currents = [fields[f:f + n] for f, n in zip(firsts, CHUNKS)]]
    unnamed x12 -> x10, local copies, waits for them, and re-layouts: 0.03 us -> 2.28 us
    pallas_call x4 -> x6, Pallas kernels: 8.48 us -> 10.5 us  [the longest x5 7.11 us: call(): pl.pallas_call(kernel, grid=grid, in_specs=[pl.BlockSpec(memory_space=plt...]
  transfers between devices with their start and end apart: 8 -> 6, of which waited for: 3 -> 4; matrix products, arithmetic and copies ran while one was open for 1% -> 1% of each run, Pallas kernels for 3% -> 7%
where the time goes in v2:
time: 93.6 us; the launch traced here: 93.4 us
  blocking collectives  52.2 us (56%)
  waiting for transfers between devices  19.7 us (21%)
  Pallas kernels  10.5 us (11%)
  starting transfers between devices  7.21 us (8%)
  local copies, waits for them, and re-layouts  2.28 us (2%)
    all_to_all x1, blocking collectives, body(): lax.all_to_all(mine.reshape(256, 1, count * 256), ('side', 'brick'), spli...  52.2 us
    ppermute x6, waiting for transfers between devices, body(): send = lambda x, route: lax.ppermute(x, 'brick', route)  19.7 us
    ppermute x6, starting transfers between devices, body(): send = lambda x, route: lax.ppermute(x, 'brick', route)  7.21 us
    pallas_call x5, Pallas kernels, call(): pl.pallas_call(kernel, grid=grid, in_specs=[pl.BlockSpec(memory_space=plt...  7.11 us
    pallas_call x1, Pallas kernels, accumulate(): pl.pallas_call(functools.partial(accumulate_kernel, count, xb), grid=(nx...  3.38 us
    unnamed x10, local copies, waits for them, and re-layouts  2.28 us
  transfers between devices with their start and end apart: 6, of which 4 were waited for; matrix products, arithmetic and copies ran while one was open for 1% of the time, Pallas kernels for 7%

profile of v2, /device:TPU:1, one launch (start us, length us, event | category | flops | bytes accessed | tf_op | source)
XLA Modules:
  0.0 93.4 jit_solution(11380866454144194231)
XLA Ops:
  0.6 3.3 %collective-permute-start.1 = (f32[5,256,256]{2,1,0:T(8,128)}, f32[5,256,256]{2,1,0:T(8,128)S(1)}, u32[]{:S(2)}, u32[]{:S(2)}) collective-permute-start(f32[5,256,256]{2,1,0:T(8,128)} %bitcast.17), channel_id=1, source_target_pairs={{0,1},{1,0},{2,3},{3,2},{4,5},{5,4},{6,7},{7,6},{8,9},{9,8},{10,11... | collective-permute-start | bytes 3932168 | tf_op jit(solution)/shard_map/ppermute | solution.py:249
  4.0 1.9 %collective-permute-start.2 = (f32[5,256,256]{2,1,0:T(8,128)}, f32[5,256,256]{2,1,0:T(8,128)S(1)}, u32[]{:S(2)}, u32[]{:S(2)}) collective-permute-start(f32[5,256,256]{2,1,0:T(8,128)} %bitcast.18), channel_id=1, source_target_pairs={{1,2},{3,4},{5,6},{7,8},{9,10},{11,12},{13,14},{15,16},{17,18},{19... | collective-permute-start | bytes 3932168 | tf_op jit(solution)/shard_map/ppermute | solution.py:249
  5.9 0.1 collective-permute-start
  6.0 0.1 add_convert_fusion
  6.1 0.7 pad_maximum_fusion.table_ref
  6.8 0.9 collective-permute-done.near_source_ref
  7.7 0.0 collective-permute-done.1.near_ref
  7.7 0.0 copy-start.1
  7.7 1.3 %copy-done.1 = f32[5,1,256,256]{3,2,1,0:T(8,128)S(1)} copy-done((f32[5,1,256,256]{3,2,1,0:T(8,128)S(1)}, f32[5,1,256,256]{3,2,1,0:T(8,128)}, u32[]{:S(2)}) %copy-start.1) | copy-done | bytes 1310744
  9.0 0.0 copy-start.4
  9.0 0.9 %copy-done.4 = f32[1,256,256]{2,1,0:T(8,128)S(1)} copy-done((f32[1,256,256]{2,1,0:T(8,128)S(1)}, f32[1,256,256]{2,1,0:T(8,128)}, u32[]{:S(2)}) %copy-start.4) | copy-done | bytes 262168
  10.0 2.1 %send_planes.1 = (f32[2560,128]{1,0:T(8,128)S(1)}, f32[5,256,256]{2,1,0:T(8,128)S(1)}, f32[5,256,256]{2,1,0:T(8,128)S(1)}, f32[256,256]{1,0:T(8,128)S(1)}) custom-call(f32[19]{0:T(128)S(1)} %pad_maximum_fusion.table_ref, f32[5,256,256]{2,1,0:T(8,128)S(1)} %bitcast.19, f32[256,256]{1,0:T(8,128)S(1)} %bitcast.23, ...), custom_call_target="tpu_custom_call" | custom-call | flops 5120 | bytes 5120 | tf_op jit(solution)/shard_map/send_planes/pallas_call | solution.py:164
  12.1 1.3 %collective-permute-start.5 = (f32[2560,128]{1,0:T(8,128)S(1)}, f32[2560,128]{1,0:T(8,128)S(1)}, u32[]{:S(2)}, u32[]{:S(2)}) collective-permute-start(f32[2560,128]{1,0:T(8,128)S(1)} %get-tuple-element.19), channel_id=1, source_target_pairs={{0,2},{2,4},{4,6},{6,8},{8,10},{10,12},{12,14},{14,16},{16,18},{18... | collective-permute-start | bytes 3932168 | tf_op jit(solution)/shard_map/ppermute | solution.py:249
  13.4 16.2 %collective-permute-done.2.raw_far_ref.far_ref = f32[5,256,256]{2,1,0:T(8,128)S(1)} collective-permute-done((f32[5,256,256]{2,1,0:T(8,128)}, f32[5,256,256]{2,1,0:T(8,128)S(1)}, u32[]{:S(2)}, u32[]{:S(2)}) %collective-permute-start.2) | collective-permute-done | bytes 1310752 | tf_op jit(solution)/shard_map/ppermute | solution.py:249
  29.7 0.7 first_step.1
  30.4 0.1 collective-permute-start.3
  30.5 0.5 collective-permute-start.4
  31.0 1.7 %far_step.1.far_part_ref = f32[5,256,256]{2,1,0:T(8,128)S(1)} custom-call(f32[19]{0:T(128)S(1)} %pad_maximum_fusion.table_ref, f32[5,256,256]{2,1,0:T(8,128)S(1)} %get-tuple-element.15.raw_ref, f32[5,256,256]{2,1,0:T(8,128)S(1)} %collective-permute-done.2.raw_far_ref.far_ref), custom_call_target="tpu_custom_call" | custom-call | flops 5120 | bytes 5120 | tf_op jit(solution)/shard_map/far_step/pallas_call | solution.py:164
  32.7 0.8 collective-permute-done.4.refs_3_
  33.5 0.0 collective-permute-done.3.refs_1_
  33.5 1.8 %second_step.1.first_ref = f32[2560,128]{1,0:T(8,128)S(1)} custom-call(f32[19]{0:T(128)S(1)} %pad_maximum_fusion.table_ref, f32[256,256]{1,0:T(8,128)S(1)} %get-tuple-element.14.source_ref, f32[5,256,256]{2,1,0:T(8,128)S(1)} %far_step.1.far_part_ref, f32[3,256,256]{2,1,0:T(8,128)S(1)} %get-tuple-element.17.refs_0_, ...), custom_call_target="tpu_custom_call" | custom-call | flops 5120 | bytes 5120 | tf_op jit(solution)/shard_map/second_step/pallas_call | solution.py:164
  35.3 1.8 %collective-permute-done.5.second_ref = f32[2560,128]{1,0:T(8,128)S(1)} collective-permute-done((f32[2560,128]{1,0:T(8,128)S(1)}, f32[2560,128]{1,0:T(8,128)S(1)}, u32[]{:S(2)}, u32[]{:S(2)}) %collective-permute-start.5) | collective-permute-done | bytes 1310752 | tf_op jit(solution)/shard_map/ppermute | solution.py:249
  37.1 0.0 copy-start.2
  37.1 0.0 copy-start.3
  37.1 0.7 add_beyond.1
  37.9 0.0 copy-start
  37.9 52.2 %all_to_all.5 = f32[256,1,1280]{2,1,0:T(1,128)S(1)} all-to-all(f32[256,1,1280]{2,1,0:T(1,128)S(1)} %bitcast.14), channel_id=1, replica_groups=mesh['side'=2,'brick'=128] {'side','brick'}, dimensions={0} | all-to-all | bytes 2621440 | tf_op jit(solution)/shard_map/all_to_all | solution.py:271
  90.0 0.0 copy-done.2
  90.1 0.0 copy-done.3
  90.1 0.0 copy-done
  90.1 3.4 %accumulate.1 = (f32[10,256,128]{2,1,0:T(8,128)}, f32[10,256,128]{2,1,0:T(8,128)}, f32[16,256,128]{2,1,0:T(8,128)}, f32[16,256,128]{2,1,0:T(8,128)}) custom-call(f32[2,1280,128]{2,1,0:T(8,128)S(1)} %bitcast.15, f32[10,256,128]{2,1,0:T(8,128)S(1)} %bitcast.20, f32[10,256,128]{2,1,0:T(8,128)S(1)} %bitcast.21, f32[16,256,128]{2,1,0:T(8,128)S(1)} %bitcast.16), custom_call_target="tpu_custom_call" | custom-call | flops 13107200 | bytes 13631488 | tf_op jit(solution)/shard_map/accumulate/pallas_call | solution.py:216
Async XLA Ops:
  0.6 7.1 %collective-permute-start.1 = (f32[5,256,256]{2,1,0:T(8,128)}, f32[5,256,256]{2,1,0:T(8,128)S(1)}, u32[]{:S(2)}, u32[]{:S(2)}) collective-permute-start(f32[5,256,256]{2,1,0:T(8,128)} %bitcast.17), channel_id=1, source_target_pairs={{0,1},{1,0},{2,3},{3,2},{4,5},{5,4},{6,7},{7,6},{8,9},{9,8},{10,11... | collective-permute-start | bytes 3932168 | tf_op jit(solution)/shard_map/ppermute | solution.py:249
  4.0 25.7 %collective-permute-start.2 = (f32[5,256,256]{2,1,0:T(8,128)}, f32[5,256,256]{2,1,0:T(8,128)S(1)}, u32[]{:S(2)}, u32[]{:S(2)}) collective-permute-start(f32[5,256,256]{2,1,0:T(8,128)} %bitcast.18), channel_id=1, source_target_pairs={{1,2},{3,4},{5,6},{7,8},{9,10},{11,12},{13,14},{15,16},{17,18},{19... | collective-permute-start | bytes 3932168 | tf_op jit(solution)/shard_map/ppermute | solution.py:249
  5.9 1.8 %collective-permute-start = (f32[256,256]{1,0:T(8,128)}, f32[256,256]{1,0:T(8,128)S(1)}, u32[]{:S(2)}, u32[]{:S(2)}) collective-permute-start(f32[256,256]{1,0:T(8,128)} %bitcast.22), channel_id=1, source_target_pairs={{0,1},{1,0},{2,3},{3,2},{4,5},{5,4},{6,7},{7,6},{8,9},{9,8},{10,11... | collective-permute-start | bytes 786440 | tf_op jit(solution)/shard_map/ppermute | solution.py:249
  7.7 1.3 %copy-start.1 = (f32[5,1,256,256]{3,2,1,0:T(8,128)S(1)}, f32[5,1,256,256]{3,2,1,0:T(8,128)}, u32[]{:S(2)}) copy-start(f32[5,1,256,256]{3,2,1,0:T(8,128)} %param.7) | copy-start | bytes 3932164
  9.0 0.9 %copy-start.4 = (f32[1,256,256]{2,1,0:T(8,128)S(1)}, f32[1,256,256]{2,1,0:T(8,128)}, u32[]{:S(2)}) copy-start(f32[1,256,256]{2,1,0:T(8,128)} %param.8) | copy-start | bytes 786436
  12.1 25.0 %collective-permute-start.5 = (f32[2560,128]{1,0:T(8,128)S(1)}, f32[2560,128]{1,0:T(8,128)S(1)}, u32[]{:S(2)}, u32[]{:S(2)}) collective-permute-start(f32[2560,128]{1,0:T(8,128)S(1)} %get-tuple-element.19), channel_id=1, source_target_pairs={{0,2},{2,4},{4,6},{6,8},{8,10},{10,12},{12,14},{14,16},{16,18},{18... | collective-permute-start | bytes 3932168 | tf_op jit(solution)/shard_map/ppermute | solution.py:249
  30.4 3.1 %collective-permute-start.3 = (f32[3,256,256]{2,1,0:T(8,128)S(1)}, f32[3,256,256]{2,1,0:T(8,128)S(1)}, u32[]{:S(2)}, u32[]{:S(2)}) collective-permute-start(f32[3,256,256]{2,1,0:T(8,128)S(1)} %get-tuple-element.17.refs_0_), channel_id=1, source_target_pairs={{0,1},{1,0},{2,3},{3,2},{4,5},{5,4},{6,7},{7,6},{8,9},{9,8},{10,11... | collective-permute-start | bytes 2359304 | tf_op jit(solution)/shard_map/ppermute | solution.py:249
  30.5 3.0 %collective-permute-start.4 = (f32[2,256,256]{2,1,0:T(8,128)S(1)}, f32[2,256,256]{2,1,0:T(8,128)S(1)}, u32[]{:S(2)}, u32[]{:S(2)}) collective-permute-start(f32[2,256,256]{2,1,0:T(8,128)S(1)} %get-tuple-element.18.refs_2_), channel_id=1, source_target_pairs={{0,1},{1,0},{2,3},{3,2},{4,5},{5,4},{6,7},{7,6},{8,9},{9,8},{10,11... | collective-permute-start | bytes 1572872 | tf_op jit(solution)/shard_map/ppermute | solution.py:249
  37.1 52.9 %copy-start.2 = (f32[10,128,1,256]{3,2,1,0:T(1,128)S(1)}, f32[10,128,1,256]{3,2,1,0:T(1,128)}, u32[]{:S(2)}) copy-start(f32[10,128,1,256]{3,2,1,0:T(1,128)} %param.11) | copy-start | bytes 3932164
  37.1 52.9 %copy-start.3 = (f32[10,128,1,256]{3,2,1,0:T(1,128)S(1)}, f32[10,128,1,256]{3,2,1,0:T(1,128)}, u32[]{:S(2)}) copy-start(f32[10,128,1,256]{3,2,1,0:T(1,128)} %param.12) | copy-start | bytes 3932164
  37.9 52.2 %copy-start = (f32[16,128,1,256]{3,2,1,0:T(1,128)S(1)}, f32[16,128,1,256]{3,2,1,0:T(1,128)}, u32[]{:S(2)}) copy-start(f32[16,128,1,256]{3,2,1,0:T(1,128)} %param.13) | copy-start | bytes 6291460

commit v3 on v2

--- a/solution.py
+++ b/solution.py
@@ -69,29 +69,32 @@
         out_ref[pl.ds(start, new.shape[0], stride=pitch), :] = new[:, h * 128 : (h + 1) * 128]
 
 
-def send_kernel(
-    table_ref, raw_ref, source_ref, near_source_ref, near_ref, out_ref, partial_ref, copy_ref, source_copy_ref
-):
-    m = pl.program_id(0)
-    weights = weights_of(table_ref, m)
-    far_w, amplitude = weights[2], weights[7]
-    count, ny, nz = copy_ref.shape
+def send_kernel(table_ref, source_ref, *refs):
+    pieces, (out_ref, partial_ref, source_copy_ref) = refs[:-3], refs[-3:]
+    count, ny, nz = partial_ref.shape
     for r in range(0, ny, ROWS):
-        raw = raw_ref[0, r : r + ROWS, :]
-        rest = far_w * raw + amplitude * near_source_ref[r : r + ROWS, :]
-        store_strips(out_ref, m, count, r, far_w * rest)
-        copy_ref[m, r : r + ROWS, :] = raw
-
-    def store(r, new):
-        partial_ref[m, r : r + ROWS, :] = new
-
-    rest = lambda r, n: amplitude * source_ref[r : r + n, :]
-    step_plane((ny, nz), weights, reader(raw_ref, 0), reader(near_ref, m), rest, store)
-
-    @pl.when(m == 0)
-    def _():
-        for r in range(0, ny, ROWS):
-            source_copy_ref[r : r + ROWS, :] = source_ref[r : r + ROWS, :]
+        source_copy_ref[r : r + ROWS, :] = source_ref[r : r + ROWS, :]
+    first = 0
+    for raw_ref, near_ref in zip(pieces[::2], pieces[1::2]):
+
+        def one_member(j, carry, raw_ref=raw_ref, near_ref=near_ref, first=first):
+            m = first + j
+            weights = weights_of(table_ref, m)
+            near_w, amplitude = weights[1], weights[7]
+            for r in range(0, ny, ROWS):
+                rows = slice(r, r + ROWS)
+                rest = near_w * near_ref[j, rows, :] + amplitude * source_ref[rows, :]
+                store_strips(out_ref, m, count, r, near_w * rest)
+
+            def store(r, new):
+                partial_ref[m, r : r + ROWS, :] = new
+
+            rest = lambda r, n: amplitude * source_ref[r : r + n, :]
+            step_plane((ny, nz), weights, reader(raw_ref, j), reader(near_ref, j), rest, store)
+            return carry
+
+        lax.fori_loop(0, raw_ref.shape[0], one_member, 0)
+        first += raw_ref.shape[0]
 
 
 def first_kernel(table_ref, partial_ref, far_ref, *out_refs):
@@ -111,20 +114,27 @@
         first += out_ref.shape[0]
 
 
-def far_kernel(table_ref, raw_ref, raw_far_ref, out_ref):
+def far_kernel(table_ref, raw_far_ref, *refs):
+    pieces, out_ref = refs[:-1], refs[-1]
     inside = table_ref[18] > 0.0
-
-    def one_member(m, carry):
-        weights = weights_of(table_ref, m)
-        far_w = weights[2]
-
-        def store(r, new):
-            out_ref[m, r : r + ROWS, :] = jnp.where(inside, far_w * new, 0.0)
-
-        step_plane(raw_ref.shape[1:], weights, reader(raw_far_ref, m), reader(raw_ref, m), lambda r, n: 0.0, store)
-        return carry
-
-    lax.fori_loop(0, raw_ref.shape[0], one_member, 0)
+    first = 0
+    for raw_ref in pieces:
+
+        def one_member(j, carry, raw_ref=raw_ref, first=first):
+            m = first + j
+            weights = weights_of(table_ref, m)
+            far_w = weights[2]
+
+            def store(r, new):
+                out_ref[m, r : r + ROWS, :] = jnp.where(inside, far_w * new, 0.0)
+
+            step_plane(
+                out_ref.shape[1:], weights, reader(raw_far_ref, m), reader(raw_ref, j), lambda r, n: 0.0, store
+            )
+            return carry
+
+        lax.fori_loop(0, raw_ref.shape[0], one_member, 0)
+        first += raw_ref.shape[0]
 
 
 def second_kernel(table_ref, source_ref, far_part_ref, *refs):
@@ -159,15 +169,13 @@
     lax.fori_loop(0, out_ref.shape[0] // rows, some_rows, 0)
 
 
-def call(kernel, name, table, arrays, out_shapes, cells, scratch=(), grid=(), in_specs=None):
+def call(kernel, name, table, arrays, out_shapes, cells):
     whole = pl.BlockSpec(memory_space=pltpu.VMEM)
     return pl.pallas_call(
         kernel,
-        grid=grid,
-        in_specs=[pl.BlockSpec(memory_space=pltpu.SMEM)] + (in_specs or [whole] * len(arrays)),
+        in_specs=[pl.BlockSpec(memory_space=pltpu.SMEM)] + [whole] * len(arrays),
         out_specs=[whole] * len(out_shapes),
         out_shape=[jax.ShapeDtypeStruct(shape, jnp.float32) for shape in out_shapes],
-        scratch_shapes=scratch,
         compiler_params=pltpu.CompilerParams(vmem_limit_bytes=32 * 1024 * 1024),
         cost_estimate=pl.CostEstimate(flops=cells // 64, bytes_accessed=cells // 64, transcendentals=0),
         name=name,
@@ -232,13 +240,12 @@
     near = [(i, i ^ 1) for i in range(count)]
     far = [(i, i + 1) for i in range(1, count - 1, 2)]
     far += [(j, i) for i, j in far]
-    second = [(i, i + 2) for i in range(0, count - 2, 2)] + [(i, i - 2) for i in range(3, count, 2)]
-    return near, far, second
+    return near, far
 
 
 def body(fields, source_field, params_a, params_b, running_means, running_squares, running_cross):
     bricks = lax.axis_size("brick")
-    near_route, far_route, second_route = routes(bricks)
+    near_route, far_route = routes(bricks)
     brick = lax.axis_index("brick")
     count = fields.shape[0]
     inside = (brick > 0) & (brick < bricks - 1)
@@ -248,24 +255,20 @@
     source = source_field[0]
     send = lambda x, route: lax.ppermute(x, "brick", route)
     ny, nz = source.shape
-    near_source = send(source, near_route)
+    half = (count + 1) // 2
+    halves = (raw[:half], raw[half:])
+    flat_shape = (raw.size // 128, 128)
     far = send(raw, far_route)
-    near = send(raw, near_route)
-    plane = lambda index: pl.BlockSpec((1, ny, nz), index)
-    flat_shape = (raw.size // 128, 128)
-    flat_plane = pl.BlockSpec((ny, nz), lambda m: (0, 0))
-    beyond, partial, raw, source = call(
-        send_kernel, "send_planes", table, (raw, source, near_source, near),
-        (flat_shape, raw.shape, raw.shape, source.shape), raw.size, grid=(count,),
-        in_specs=[plane(lambda m: (m, 0, 0)), flat_plane, flat_plane, pl.BlockSpec(memory_space=pltpu.VMEM)],
-    )
-    beyond = send(beyond, second_route)
-    half = (count + 1) // 2
+    pairs = [x for piece in halves for x in (piece, send(piece, near_route))]
+    beyond, partial, source = call(
+        send_kernel, "send_planes", table, (source, *pairs), (flat_shape, raw.shape, source.shape), raw.size
+    )
+    beyond = send(beyond, far_route)
     ahead = call(
-        first_kernel, "first_step", table, (partial, far), ((half, ny, nz), (count - half, ny, nz)), raw.size
+        first_kernel, "first_step", table, (partial, far), [piece.shape for piece in halves], raw.size
     )
     pairs = [x for piece in ahead for x in (piece, send(piece, near_route))]
-    (far_part,) = call(far_kernel, "far_step", table, (raw, far), (raw.shape,), raw.size)
+    (far_part,) = call(far_kernel, "far_step", table, (far, *halves), (raw.shape,), raw.size)
     (mine,) = call(second_kernel, "second_step", table, (source, far_part, *pairs), (flat_shape,), raw.size)
     (mine,) = call(add_kernel, "add_beyond", table, (mine, beyond), (flat_shape,), raw.size // 8)
     strips = lax.all_to_all(

time: 93.6 us -> 93 us (level)
  waiting for transfers between devices: 19.7 us -> 14.7 us
  starting transfers between devices: 7.21 us -> 9.32 us
  blocking collectives: 52.2 us -> 53.8 us
  local copies, waits for them, and re-layouts: 2.28 us -> 3.27 us
    ppermute x6, waiting for transfers between devices: 19.7 us -> 14.7 us  [body(): send = lambda x, route: lax.ppermute(x, 'brick', route)]
    slice x0 -> x2, local copies, waits for them, and re-layouts: none -> 2.29 us  [body(): halves = (raw[:half], raw[half:])]
    ppermute x6, starting transfers between devices: 7.21 us -> 9.32 us  [body(): send = lambda x, route: lax.ppermute(x, 'brick', route)]
    all_to_all x1, blocking collectives: 52.2 us -> 53.8 us  [body(): lax.all_to_all(mine.reshape(256, 1, count * 256), ('side', 'brick'), spli...]
    unnamed x10 -> x12, local copies, waits for them, and re-layouts: 2.28 us -> 0.97 us
  transfers between devices with their start and end apart: 6 -> 6, of which waited for: 4 -> 4; matrix products, arithmetic and copies ran while one was open for 1% -> 3% of each run, Pallas kernels for 7% -> 7%
where the time goes in v3:
time: 93 us; the launch traced here: 92.7 us
  blocking collectives  53.8 us (58%)
  waiting for transfers between devices  14.7 us (16%)
  Pallas kernels  10.7 us (12%)
  starting transfers between devices  9.32 us (10%)
  local copies, waits for them, and re-layouts  3.27 us (4%)
    all_to_all x1, blocking collectives, body(): lax.all_to_all(mine.reshape(256, 1, count * 256), ('side', 'brick'), spli...  53.8 us
    ppermute x6, waiting for transfers between devices, body(): send = lambda x, route: lax.ppermute(x, 'brick', route)  14.7 us
    ppermute x6, starting transfers between devices, body(): send = lambda x, route: lax.ppermute(x, 'brick', route)  9.32 us
    pallas_call x5, Pallas kernels, call(): pl.pallas_call(kernel, in_specs=[pl.BlockSpec(memory_space=pltpu.SMEM)] +...  7.35 us
    pallas_call x1, Pallas kernels, accumulate(): pl.pallas_call(functools.partial(accumulate_kernel, count, xb), grid=(nx...  3.38 us
    slice x2, local copies, waits for them, and re-layouts, body(): halves = (raw[:half], raw[half:])  2.29 us
  transfers between devices with their start and end apart: 6, of which 4 were waited for; matrix products, arithmetic and copies ran while one was open for 3% of the time, Pallas kernels for 7%

profile of v3, /device:TPU:1, one launch (start us, length us, event | category | flops | bytes accessed | tf_op | source)
XLA Modules:
  0.0 92.7 jit_solution(6092559980194112269)
XLA Ops:
  0.6 4.6 %collective-permute-start.2 = (f32[5,256,256]{2,1,0:T(8,128)}, f32[5,256,256]{2,1,0:T(8,128)S(1)}, u32[]{:S(2)}, u32[]{:S(2)}) collective-permute-start(f32[5,256,256]{2,1,0:T(8,128)} %bitcast.25), channel_id=1, source_target_pairs={{1,2},{3,4},{5,6},{7,8},{9,10},{11,12},{13,14},{15,16},{17,18},{19... | collective-permute-start | bytes 3932168 | tf_op jit(solution)/shard_map/ppermute | solution.py:256
  5.2 0.0 copy-start.4
  5.2 0.0 copy-start.5
  5.3 1.2 %slice_bitcast_fusion.refs_0_ = f32[3,256,256]{2,1,0:T(8,128)S(1)} fusion(f32[5,1,256,256]{3,2,0,1:T(8,128)} %bitcast.26), kind=kLoop, calls=%fused_computation | loop fusion | bytes 1572864 | tf_op jit(solution)/shard_map/slice | solution.py:259
  6.5 0.1 collective-permute-start
  6.6 1.1 %slice_bitcast_fusion.1.refs_2_.refs_1_ = f32[2,256,256]{2,1,0:T(8,128)S(1)} fusion(f32[5,1,256,256]{3,2,0,1:T(8,128)} %bitcast.27), kind=kLoop, calls=%fused_computation.1 | loop fusion | bytes 1048576 | tf_op jit(solution)/shard_map/slice | solution.py:259
  7.7 0.6 collective-permute-start.1
  8.2 0.1 add_convert_fusion
  8.3 0.0 copy-done.4
  8.3 0.0 copy-done.5
  8.3 0.1 pad_maximum_fusion.table_ref
  8.4 1.5 %collective-permute-done.1.refs_3_ = f32[2,256,256]{2,1,0:T(8,128)} collective-permute-done((f32[2,256,256]{2,1,0:T(8,128)S(1)}, f32[2,256,256]{2,1,0:T(8,128)}, u32[]{:S(2)}, u32[]{:S(2)}) %collective-permute-start.1) | collective-permute-done | bytes 524320 | tf_op jit(solution)/shard_map/ppermute | solution.py:256
  9.9 0.0 collective-permute-done.refs_1_
  9.9 0.0 copy-start.3
  9.9 0.9 %copy-done.3 = f32[1,256,256]{2,1,0:T(8,128)S(1)} copy-done((f32[1,256,256]{2,1,0:T(8,128)S(1)}, f32[1,256,256]{2,1,0:T(8,128)}, u32[]{:S(2)}) %copy-start.3) | copy-done | bytes 262168
  10.9 2.4 %send_planes.1 = (f32[2560,128]{1,0:T(8,128)S(1)}, f32[5,256,256]{2,1,0:T(8,128)S(1)}, f32[256,256]{1,0:T(8,128)S(1)}) custom-call(f32[19]{0:T(128)S(1)} %pad_maximum_fusion.table_ref, f32[256,256]{1,0:T(8,128)S(1)} %bitcast.24, f32[3,256,256]{2,1,0:T(8,128)S(1)} %slice_bitcast_fusion.refs_0_, f32[3,256,256]{2,1,0:T(8,128)S(1)} %collective-permute-done.refs_1_, ...), custom_call_target="tpu_custom_call" | custom-call | flops 5120 | bytes 5120 | tf_op jit(solution)/shard_map/send_planes/pallas_call | solution.py:174
  13.3 3.5 %collective-permute-start.5 = (f32[2560,128]{1,0:T(8,128)S(1)}, f32[2560,128]{1,0:T(8,128)S(1)}, u32[]{:S(2)}, u32[]{:S(2)}) collective-permute-start(f32[2560,128]{1,0:T(8,128)S(1)} %get-tuple-element.17), channel_id=1, source_target_pairs={{1,2},{3,4},{5,6},{7,8},{9,10},{11,12},{13,14},{15,16},{17,18},{19... | collective-permute-start | bytes 3932168 | tf_op jit(solution)/shard_map/ppermute | solution.py:256
  16.7 4.0 %collective-permute-done.2.raw_far_ref.far_ref = f32[5,256,256]{2,1,0:T(8,128)S(1)} collective-permute-done((f32[5,256,256]{2,1,0:T(8,128)}, f32[5,256,256]{2,1,0:T(8,128)S(1)}, u32[]{:S(2)}, u32[]{:S(2)}) %collective-permute-start.2) | collective-permute-done | bytes 1310752 | tf_op jit(solution)/shard_map/ppermute | solution.py:256
  20.7 0.7 first_step.1
  21.5 0.1 collective-permute-start.3
  21.6 0.5 collective-permute-start.4
  22.1 1.7 %far_step.1.far_part_ref = f32[5,256,256]{2,1,0:T(8,128)S(1)} custom-call(f32[19]{0:T(128)S(1)} %pad_maximum_fusion.table_ref, f32[5,256,256]{2,1,0:T(8,128)S(1)} %collective-permute-done.2.raw_far_ref.far_ref, f32[3,256,256]{2,1,0:T(8,128)S(1)} %slice_bitcast_fusion.refs_0_, f32[2,256,256]{2,1,0:T(8,128)S(1)} %slice_bitcast_fusion.1.refs_2_.refs_1_), custom_call_target="tpu_custom_call" | custom-call | flops 5120 | bytes 5120 | tf_op jit(solution)/shard_map/far_step/pallas_call | solution.py:174
  23.7 0.8 collective-permute-done.4.refs_3_
  24.6 0.0 collective-permute-done.3.refs_1_
  24.6 1.8 %second_step.1.first_ref = f32[2560,128]{1,0:T(8,128)S(1)} custom-call(f32[19]{0:T(128)S(1)} %pad_maximum_fusion.table_ref, f32[256,256]{1,0:T(8,128)S(1)} %get-tuple-element.13.source_ref, f32[5,256,256]{2,1,0:T(8,128)S(1)} %far_step.1.far_part_ref, f32[3,256,256]{2,1,0:T(8,128)S(1)} %get-tuple-element.15.refs_0_, ...), custom_call_target="tpu_custom_call" | custom-call | flops 5120 | bytes 5120 | tf_op jit(solution)/shard_map/second_step/pallas_call | solution.py:174
  26.4 8.4 %collective-permute-done.5.second_ref = f32[2560,128]{1,0:T(8,128)S(1)} collective-permute-done((f32[2560,128]{1,0:T(8,128)S(1)}, f32[2560,128]{1,0:T(8,128)S(1)}, u32[]{:S(2)}, u32[]{:S(2)}) %collective-permute-start.5) | collective-permute-done | bytes 1310752 | tf_op jit(solution)/shard_map/ppermute | solution.py:256
  34.8 0.0 copy-start.1
  34.8 0.0 copy-start.2
  34.8 0.7 add_beyond.1
  35.5 0.0 copy-start
  35.5 53.8 %all_to_all.5 = f32[256,1,1280]{2,1,0:T(1,128)S(1)} all-to-all(f32[256,1,1280]{2,1,0:T(1,128)S(1)} %bitcast.19), channel_id=1, replica_groups=mesh['side'=2,'brick'=128] {'side','brick'}, dimensions={0} | all-to-all | bytes 2621440 | tf_op jit(solution)/shard_map/all_to_all | solution.py:274
  89.3 0.0 copy-done.1
  89.3 0.0 copy-done.2
  89.3 0.0 copy-done
  89.3 3.4 %accumulate.1 = (f32[10,256,128]{2,1,0:T(8,128)}, f32[10,256,128]{2,1,0:T(8,128)}, f32[16,256,128]{2,1,0:T(8,128)}, f32[16,256,128]{2,1,0:T(8,128)}) custom-call(f32[2,1280,128]{2,1,0:T(8,128)S(1)} %bitcast.20, f32[10,256,128]{2,1,0:T(8,128)S(1)} %bitcast.22, f32[10,256,128]{2,1,0:T(8,128)S(1)} %bitcast.23, f32[16,256,128]{2,1,0:T(8,128)S(1)} %bitcast.21), custom_call_target="tpu_custom_call" | custom-call | flops 13107200 | bytes 13631488 | tf_op jit(solution)/shard_map/accumulate/pallas_call | solution.py:224
Async XLA Ops:
  0.6 20.1 %collective-permute-start.2 = (f32[5,256,256]{2,1,0:T(8,128)}, f32[5,256,256]{2,1,0:T(8,128)S(1)}, u32[]{:S(2)}, u32[]{:S(2)}) collective-permute-start(f32[5,256,256]{2,1,0:T(8,128)} %bitcast.25), channel_id=1, source_target_pairs={{1,2},{3,4},{5,6},{7,8},{9,10},{11,12},{13,14},{15,16},{17,18},{19... | collective-permute-start | bytes 3932168 | tf_op jit(solution)/shard_map/ppermute | solution.py:256
  5.2 3.1 %copy-start.4 = (f32[8]{0:T(128)S(1)}, f32[8]{0:T(128)}, u32[]{:S(2)}) copy-start(f32[8]{0:T(128)} %param.10) | copy-start | bytes 100
  5.2 3.1 %copy-start.5 = (f32[8]{0:T(128)S(1)}, f32[8]{0:T(128)}, u32[]{:S(2)}) copy-start(f32[8]{0:T(128)} %param.9) | copy-start | bytes 100
  6.5 3.4 %collective-permute-start = (f32[3,256,256]{2,1,0:T(8,128)S(1)}, f32[3,256,256]{2,1,0:T(8,128)S(1)}, u32[]{:S(2)}, u32[]{:S(2)}) collective-permute-start(f32[3,256,256]{2,1,0:T(8,128)S(1)} %slice_bitcast_fusion.refs_0_), channel_id=1, source_target_pairs={{0,1},{1,0},{2,3},{3,2},{4,5},{5,4},{6,7},{7,6},{8,9},{9,8},{10,11... | collective-permute-start | bytes 2359304 | tf_op jit(solution)/shard_map/ppermute | solution.py:256
  7.7 2.2 %collective-permute-start.1 = (f32[2,256,256]{2,1,0:T(8,128)S(1)}, f32[2,256,256]{2,1,0:T(8,128)}, u32[]{:S(2)}, u32[]{:S(2)}) collective-permute-start(f32[2,256,256]{2,1,0:T(8,128)S(1)} %slice_bitcast_fusion.1.refs_2_.refs_1_), channel_id=1, source_target_pairs={{0,1},{1,0},{2,3},{3,2},{4,5},{5,4},{6,7},{7,6},{8,9},{9,8},{10,11... | collective-permute-start | bytes 1572872 | tf_op jit(solution)/shard_map/ppermute | solution.py:256
  9.9 1.0 %copy-start.3 = (f32[1,256,256]{2,1,0:T(8,128)S(1)}, f32[1,256,256]{2,1,0:T(8,128)}, u32[]{:S(2)}) copy-start(f32[1,256,256]{2,1,0:T(8,128)} %param.8) | copy-start | bytes 786436
  13.3 21.5 %collective-permute-start.5 = (f32[2560,128]{1,0:T(8,128)S(1)}, f32[2560,128]{1,0:T(8,128)S(1)}, u32[]{:S(2)}, u32[]{:S(2)}) collective-permute-start(f32[2560,128]{1,0:T(8,128)S(1)} %get-tuple-element.17), channel_id=1, source_target_pairs={{1,2},{3,4},{5,6},{7,8},{9,10},{11,12},{13,14},{15,16},{17,18},{19... | collective-permute-start | bytes 3932168 | tf_op jit(solution)/shard_map/ppermute | solution.py:256
  21.5 3.1 %collective-permute-start.3 = (f32[3,256,256]{2,1,0:T(8,128)S(1)}, f32[3,256,256]{2,1,0:T(8,128)S(1)}, u32[]{:S(2)}, u32[]{:S(2)}) collective-permute-start(f32[3,256,256]{2,1,0:T(8,128)S(1)} %get-tuple-element.15.refs_0_), channel_id=1, source_target_pairs={{0,1},{1,0},{2,3},{3,2},{4,5},{5,4},{6,7},{7,6},{8,9},{9,8},{10,11... | collective-permute-start | bytes 2359304 | tf_op jit(solution)/shard_map/ppermute | solution.py:256
  21.6 3.0 %collective-permute-start.4 = (f32[2,256,256]{2,1,0:T(8,128)S(1)}, f32[2,256,256]{2,1,0:T(8,128)S(1)}, u32[]{:S(2)}, u32[]{:S(2)}) collective-permute-start(f32[2,256,256]{2,1,0:T(8,128)S(1)} %get-tuple-element.16.refs_2_), channel_id=1, source_target_pairs={{0,1},{1,0},{2,3},{3,2},{4,5},{5,4},{6,7},{7,6},{8,9},{9,8},{10,11... | collective-permute-start | bytes 1572872 | tf_op jit(solution)/shard_map/ppermute | solution.py:256
  34.8 54.5 %copy-start.1 = (f32[10,128,1,256]{3,2,1,0:T(1,128)S(1)}, f32[10,128,1,256]{3,2,1,0:T(1,128)}, u32[]{:S(2)}) copy-start(f32[10,128,1,256]{3,2,1,0:T(1,128)} %param.11) | copy-start | bytes 3932164
  34.8 54.5 %copy-start.2 = (f32[10,128,1,256]{3,2,1,0:T(1,128)S(1)}, f32[10,128,1,256]{3,2,1,0:T(1,128)}, u32[]{:S(2)}) copy-start(f32[10,128,1,256]{3,2,1,0:T(1,128)} %param.12) | copy-start | bytes 3932164
  35.5 53.8 %copy-start = (f32[16,128,1,256]{3,2,1,0:T(1,128)S(1)}, f32[16,128,1,256]{3,2,1,0:T(1,128)}, u32[]{:S(2)}) copy-start(f32[16,128,1,256]{3,2,1,0:T(1,128)} %param.13) | copy-start | bytes 6291460

commit v4 on v3

--- a/solution.py
+++ b/solution.py
@@ -13,6 +13,7 @@
 UPPER = np.asarray((0.12, 0.12, 0.12, 0.06, 0.2, 1.0, 1.5, 0.1), np.float32)
 WIDTH = UPPER - LOWER
 ROWS = 64
+LAST = 64
 
 
 def weights_of(table_ref, m):
@@ -70,7 +71,7 @@
 
 
 def send_kernel(table_ref, source_ref, *refs):
-    pieces, (out_ref, partial_ref, source_copy_ref) = refs[:-3], refs[-3:]
+    pieces, (out_ref, last_ref, partial_ref, source_copy_ref) = refs[:-4], refs[-4:]
     count, ny, nz = partial_ref.shape
     for r in range(0, ny, ROWS):
         source_copy_ref[r : r + ROWS, :] = source_ref[r : r + ROWS, :]
@@ -84,7 +85,10 @@
             for r in range(0, ny, ROWS):
                 rows = slice(r, r + ROWS)
                 rest = near_w * near_ref[j, rows, :] + amplitude * source_ref[rows, :]
-                store_strips(out_ref, m, count, r, near_w * rest)
+                if r < ny - LAST:
+                    store_strips(out_ref, m, count, r, near_w * rest)
+                else:
+                    store_strips(last_ref, m, count, r - (ny - LAST), near_w * rest)
 
             def store(r, new):
                 partial_ref[m, r : r + ROWS, :] = new
@@ -158,76 +162,86 @@
         first += own_ref.shape[0]
 
 
-def add_kernel(table_ref, first_ref, second_ref, out_ref):
-    rows = 160
+def add_kernel(first, table_ref, into_ref, part_ref, out_ref):
+    rows = 320
 
     def some_rows(i, carry):
-        at = pl.ds(pl.multiple_of(i * rows, rows), rows)
-        out_ref[at, :] = first_ref[at, :] + second_ref[at, :]
+        start = pl.multiple_of(i * rows, rows)
+        at = pl.ds(first + start, rows)
+        out_ref[at, :] = into_ref[at, :] + part_ref[pl.ds(start, rows), :]
         return carry
 
-    lax.fori_loop(0, out_ref.shape[0] // rows, some_rows, 0)
-
-
-def call(kernel, name, table, arrays, out_shapes, cells):
+    lax.fori_loop(0, part_ref.shape[0] // rows, some_rows, 0)
+
+
+def call(kernel, name, table, arrays, out_shapes, cells, aliases={}):
     whole = pl.BlockSpec(memory_space=pltpu.VMEM)
     return pl.pallas_call(
         kernel,
         in_specs=[pl.BlockSpec(memory_space=pltpu.SMEM)] + [whole] * len(arrays),
         out_specs=[whole] * len(out_shapes),
         out_shape=[jax.ShapeDtypeStruct(shape, jnp.float32) for shape in out_shapes],
+        input_output_aliases=aliases,
         compiler_params=pltpu.CompilerParams(vmem_limit_bytes=32 * 1024 * 1024),
         cost_estimate=pl.CostEstimate(flops=cells // 64, bytes_accessed=cells // 64, transcendentals=0),
         name=name,
     )(table, *arrays)
 
 
-def accumulate_kernel(count, xb, gathered, means_ref, squares_ref, cross_ref, *outs):
-    new_means_ref, new_squares_ref, new_cross_ref, maps_ref, held = outs
-    i = pl.program_id(0)
-    rows = pl.ds(pl.multiple_of(i * 2 * xb, 2 * xb), 2 * xb)
-    for s in range(2):
-        for m in range(count):
-            for h in range(2):
-                held[s * count + m, pl.ds(h, xb, stride=2), :] = gathered[
-                    s, pl.ds(i * (xb * 2 * count) + m * 2 + h, xb, stride=2 * count), :
-                ]
-
-    def moments(m):
-        out, mean = held[m], means_ref[m, rows, :]
-        deviation = out - mean
-        new_mean = mean + deviation * (1.0 / (PRIOR + 1))
-        after = out - new_mean
-        new_square = squares_ref[m, rows, :] + deviation * after
-        new_means_ref[m] = new_mean
-        new_squares_ref[m] = new_square
-        return deviation, after, new_square
-
-    base = [moments(0), moments(1)]
-    for m in range(2, 2 * count):
-        k = m - 2
-        _, after, new_square = moments(m)
-        first_cross = cross_ref[k, rows, :] + base[1][0] * after
-        total_cross = cross_ref[8 + k, rows, :] + base[0][0] * after
-        new_cross_ref[k] = first_cross
-        new_cross_ref[8 + k] = total_cross
-        maps_ref[k] = first_cross * lax.rsqrt(base[1][2] * new_square)
-        maps_ref[8 + k] = 1.0 - total_cross * lax.rsqrt(base[0][2] * new_square)
+def accumulate_kernel(count, xb, gathered, means_ref, squares_ref, cross_ref, *refs):
+    outs, blocks, (held, copied) = refs[:4], refs[4:8], refs[8:]
+    new_means_ref, new_squares_ref, new_cross_ref, maps_ref = blocks
+    copies = []
+    for i in range(128 // xb):
+        rows = pl.ds(i * 2 * xb, 2 * xb)
+        for s in range(2):
+            for m in range(count):
+                for h in range(2):
+                    held[s * count + m, pl.ds(h, xb, stride=2), :] = gathered[
+                        s, pl.ds(i * (xb * 2 * count) + m * 2 + h, xb, stride=2 * count), :
+                    ]
+
+        def moments(m):
+            out, mean = held[m], means_ref[m, rows, :]
+            deviation = out - mean
+            new_mean = mean + deviation * (1.0 / (PRIOR + 1))
+            after = out - new_mean
+            new_square = squares_ref[m, rows, :] + deviation * after
+            new_means_ref[m, rows, :] = new_mean
+            new_squares_ref[m, rows, :] = new_square
+            return deviation, after, new_square
+
+        base = [moments(0), moments(1)]
+        for m in range(2, 2 * count):
+            k = m - 2
+            _, after, new_square = moments(m)
+            first_cross = cross_ref[k, rows, :] + base[1][0] * after
+            total_cross = cross_ref[8 + k, rows, :] + base[0][0] * after
+            new_cross_ref[k, rows, :] = first_cross
+            new_cross_ref[8 + k, rows, :] = total_cross
+            maps_ref[k, rows, :] = first_cross * lax.rsqrt(base[1][2] * new_square)
+            maps_ref[8 + k, rows, :] = 1.0 - total_cross * lax.rsqrt(base[0][2] * new_square)
+        for j, (block, out) in enumerate(zip(blocks, outs)):
+            copy = pltpu.make_async_copy(block.at[:, rows], out.at[:, rows], copied.at[i, j])
+            copy.start()
+            copies.append(copy)
+    for copy in copies:
+        copy.wait()
 
 
 def accumulate(gathered, count, means, squares, cross):
     xb = 32
     nx = 128
     whole = pl.BlockSpec(memory_space=pltpu.VMEM)
-    block = lambda lead: pl.BlockSpec((lead, 2 * xb, 128), lambda i: (0, i, 0))
-    shape = lambda lead: jax.ShapeDtypeStruct((lead, 2 * nx, 128), jnp.float32)
+    shape = lambda lead: (lead, 2 * nx, 128)
+    leads = (10, 10, 16, 16)
     return pl.pallas_call(
         functools.partial(accumulate_kernel, count, xb),
-        grid=(nx // xb,),
         in_specs=[whole] * 4,
-        out_specs=[block(10), block(10), block(16), block(16)],
-        out_shape=[shape(10), shape(10), shape(16), shape(16)],
-        scratch_shapes=[pltpu.VMEM((10, 2 * xb, 128), jnp.float32)],
+        out_specs=[pl.BlockSpec(memory_space=pl.ANY)] * 4,
+        out_shape=[jax.ShapeDtypeStruct(shape(lead), jnp.float32) for lead in leads],
+        scratch_shapes=[pltpu.VMEM(shape(lead), jnp.float32) for lead in leads]
+        + [pltpu.VMEM((10, 2 * xb, 128), jnp.float32), pltpu.SemaphoreType.DMA((nx // xb, 4))],
         compiler_params=pltpu.CompilerParams(vmem_limit_bytes=32 * 1024 * 1024),
         cost_estimate=pl.CostEstimate(
             flops=40 * 10 * nx * 256, bytes_accessed=13 * 1024 * 1024, transcendentals=16 * nx * 256
@@ -260,17 +274,23 @@
     flat_shape = (raw.size // 128, 128)
     far = send(raw, far_route)
     pairs = [x for piece in halves for x in (piece, send(piece, near_route))]
-    beyond, partial, source = call(
-        send_kernel, "send_planes", table, (source, *pairs), (flat_shape, raw.shape, source.shape), raw.size
-    )
-    beyond = send(beyond, far_route)
+    cut = (ny - LAST) * count * (nz // 128)
+    *beyond, partial, source = call(
+        send_kernel, "send_planes", table, (source, *pairs),
+        ((cut, 128), (raw.size // 128 - cut, 128), raw.shape, source.shape), raw.size,
+    )
+    beyond = [send(part, far_route) for part in beyond]
     ahead = call(
         first_kernel, "first_step", table, (partial, far), [piece.shape for piece in halves], raw.size
     )
     pairs = [x for piece in ahead for x in (piece, send(piece, near_route))]
     (far_part,) = call(far_kernel, "far_step", table, (far, *halves), (raw.shape,), raw.size)
     (mine,) = call(second_kernel, "second_step", table, (source, far_part, *pairs), (flat_shape,), raw.size)
-    (mine,) = call(add_kernel, "add_beyond", table, (mine, beyond), (flat_shape,), raw.size // 8)
+    for start, part in zip((0, cut), beyond):
+        (mine,) = call(
+            functools.partial(add_kernel, start), "add_beyond", table, (mine, part), (flat_shape,), part.size // 8,
+            aliases={1: 0},
+        )
     strips = lax.all_to_all(
         mine.reshape(256, 1, count * 256), ("side", "brick"), split_axis=0, concat_axis=0, tiled=True
     )

time: 93 us -> 92.7 us (level)
  waiting for transfers between devices: 14.7 us -> 10.4 us
  starting transfers between devices: 9.32 us -> 13 us
    ppermute x6 -> x7, waiting for transfers between devices: 14.7 us -> 10.4 us  [body(): send = lambda x, route: lax.ppermute(x, 'brick', route)]
    ppermute x6 -> x7, starting transfers between devices: 9.32 us -> 13 us  [body(): send = lambda x, route: lax.ppermute(x, 'brick', route)]
    pallas_call x5 -> x6, Pallas kernels: 7.35 us -> 7.88 us  [call(): pl.pallas_call(kernel, in_specs=[pl.BlockSpec(memory_space=pltpu.SMEM)] +...]
  transfers between devices with their start and end apart: 6 -> 7, of which waited for: 4 -> 4; matrix products, arithmetic and copies ran while one was open for 3% -> 3% of each run, Pallas kernels for 7% -> 8%
where the time goes in v4:
time: 92.7 us; the launch traced here: 92.4 us
  blocking collectives  53.8 us (58%)
  starting transfers between devices  13 us (14%)
  Pallas kernels  11.1 us (12%)
  waiting for transfers between devices  10.4 us (11%)
  local copies, waits for them, and re-layouts  3.27 us (4%)
    all_to_all x1, blocking collectives, body(): lax.all_to_all(mine.reshape(256, 1, count * 256), ('side', 'brick'), spli...  53.8 us
    ppermute x7, starting transfers between devices, body(): send = lambda x, route: lax.ppermute(x, 'brick', route)  13 us
    ppermute x7, waiting for transfers between devices, body(): send = lambda x, route: lax.ppermute(x, 'brick', route)  10.4 us
    pallas_call x6, Pallas kernels, call(): pl.pallas_call(kernel, in_specs=[pl.BlockSpec(memory_space=pltpu.SMEM)] +...  7.88 us
    pallas_call x1, Pallas kernels, accumulate(): pl.pallas_call(functools.partial(accumulate_kernel, count, xb), in_specs=...  3.19 us
    slice x2, local copies, waits for them, and re-layouts, body(): halves = (raw[:half], raw[half:])  2.29 us
  transfers between devices with their start and end apart: 7, of which 4 were waited for; matrix products, arithmetic and copies ran while one was open for 3% of the time, Pallas kernels for 8%

profile of v4, /device:TPU:1, one launch (start us, length us, event | category | flops | bytes accessed | tf_op | source)
XLA Modules:
  0.0 92.4 jit_solution(15485373010058161648)
XLA Ops:
  0.6 4.6 %collective-permute-start.2 = (f32[5,256,256]{2,1,0:T(8,128)}, f32[5,256,256]{2,1,0:T(8,128)S(1)}, u32[]{:S(2)}, u32[]{:S(2)}) collective-permute-start(f32[5,256,256]{2,1,0:T(8,128)} %bitcast.25), channel_id=1, source_target_pairs={{1,2},{3,4},{5,6},{7,8},{9,10},{11,12},{13,14},{15,16},{17,18},{19... | collective-permute-start | bytes 3932168 | tf_op jit(solution)/shard_map/ppermute | solution.py:270
  5.2 0.0 copy-start.4
  5.2 0.0 copy-start.5
  5.3 1.2 %slice_bitcast_fusion.refs_0_ = f32[3,256,256]{2,1,0:T(8,128)S(1)} fusion(f32[5,1,256,256]{3,2,0,1:T(8,128)} %bitcast.26), kind=kLoop, calls=%fused_computation | loop fusion | bytes 1572864 | tf_op jit(solution)/shard_map/slice | solution.py:273
  6.5 0.1 collective-permute-start
  6.6 1.1 %slice_bitcast_fusion.1.refs_2_.refs_1_ = f32[2,256,256]{2,1,0:T(8,128)S(1)} fusion(f32[5,1,256,256]{3,2,0,1:T(8,128)} %bitcast.27), kind=kLoop, calls=%fused_computation.1 | loop fusion | bytes 1048576 | tf_op jit(solution)/shard_map/slice | solution.py:273
  7.7 0.6 collective-permute-start.1
  8.2 0.1 add_convert_fusion
  8.3 0.0 copy-done.4
  8.3 0.0 copy-done.5
  8.3 0.1 pad_maximum_fusion.table_ref
  8.4 1.5 %collective-permute-done.1.refs_3_ = f32[2,256,256]{2,1,0:T(8,128)} collective-permute-done((f32[2,256,256]{2,1,0:T(8,128)S(1)}, f32[2,256,256]{2,1,0:T(8,128)}, u32[]{:S(2)}, u32[]{:S(2)}) %collective-permute-start.1) | collective-permute-done | bytes 524320 | tf_op jit(solution)/shard_map/ppermute | solution.py:270
  9.9 0.0 collective-permute-done.refs_1_
  9.9 0.0 copy-start.3
  9.9 0.9 %copy-done.3 = f32[1,256,256]{2,1,0:T(8,128)S(1)} copy-done((f32[1,256,256]{2,1,0:T(8,128)S(1)}, f32[1,256,256]{2,1,0:T(8,128)}, u32[]{:S(2)}) %copy-start.3) | copy-done | bytes 262168
  10.9 2.4 %send_planes.1 = (f32[1920,128]{1,0:T(8,128)S(1)}, f32[640,128]{1,0:T(8,128)S(1)}, f32[5,256,256]{2,1,0:T(8,128)S(1)}, f32[256,256]{1,0:T(8,128)S(1)}) custom-call(f32[19]{0:T(128)S(1)} %pad_maximum_fusion.table_ref, f32[256,256]{1,0:T(8,128)S(1)} %bitcast.24, f32[3,256,256]{2,1,0:T(8,128)S(1)} %slice_bitcast_fusion.refs_0_, ...), custom_call_target="tpu_custom_call" | custom-call | flops 5120 | bytes 5120 | tf_op jit(solution)/shard_map/send_planes/pallas_call | solution.py:179
  13.3 3.5 %collective-permute-start.5 = (f32[1920,128]{1,0:T(8,128)S(1)}, f32[1920,128]{1,0:T(8,128)S(1)}, u32[]{:S(2)}, u32[]{:S(2)}) collective-permute-start(f32[1920,128]{1,0:T(8,128)S(1)} %get-tuple-element.18), channel_id=1, source_target_pairs={{1,2},{3,4},{5,6},{7,8},{9,10},{11,12},{13,14},{15,16},{17,18},{19... | collective-permute-start | bytes 2949128 | tf_op jit(solution)/shard_map/ppermute | solution.py:270
  16.7 4.0 %collective-permute-done.2.raw_far_ref.far_ref = f32[5,256,256]{2,1,0:T(8,128)S(1)} collective-permute-done((f32[5,256,256]{2,1,0:T(8,128)}, f32[5,256,256]{2,1,0:T(8,128)S(1)}, u32[]{:S(2)}, u32[]{:S(2)}) %collective-permute-start.2) | collective-permute-done | bytes 1310752 | tf_op jit(solution)/shard_map/ppermute | solution.py:270
  20.7 0.7 first_step.1
  21.5 0.1 collective-permute-start.3
  21.6 0.5 collective-permute-start.4
  22.1 3.6 %collective-permute-start.6 = (f32[640,128]{1,0:T(8,128)S(1)}, f32[640,128]{1,0:T(8,128)S(1)}, u32[]{:S(2)}, u32[]{:S(2)}) collective-permute-start(f32[640,128]{1,0:T(8,128)S(1)} %get-tuple-element.19), channel_id=1, source_target_pairs={{1,2},{3,4},{5,6},{7,8},{9,10},{11,12},{13,14},{15,16},{17,18},{19... | collective-permute-start | bytes 983048 | tf_op jit(solution)/shard_map/ppermute | solution.py:270
  25.7 1.7 %far_step.1.far_part_ref = f32[5,256,256]{2,1,0:T(8,128)S(1)} custom-call(f32[19]{0:T(128)S(1)} %pad_maximum_fusion.table_ref, f32[5,256,256]{2,1,0:T(8,128)S(1)} %collective-permute-done.2.raw_far_ref.far_ref, f32[3,256,256]{2,1,0:T(8,128)S(1)} %slice_bitcast_fusion.refs_0_, f32[2,256,256]{2,1,0:T(8,128)S(1)} %slice_bitcast_fusion.1.refs_2_.refs_1_), custom_call_target="tpu_custom_call" | custom-call | flops 5120 | bytes 5120 | tf_op jit(solution)/shard_map/far_step/pallas_call | solution.py:179
  27.4 0.0 collective-permute-done.4.refs_3_
  27.4 0.0 collective-permute-done.3.refs_1_
  27.4 1.8 %second_step.1.into_ref = f32[2560,128]{1,0:T(8,128)S(1)} custom-call(f32[19]{0:T(128)S(1)} %pad_maximum_fusion.table_ref, f32[256,256]{1,0:T(8,128)S(1)} %get-tuple-element.14.source_ref, f32[5,256,256]{2,1,0:T(8,128)S(1)} %far_step.1.far_part_ref, f32[3,256,256]{2,1,0:T(8,128)S(1)} %get-tuple-element.16.refs_0_, ...), custom_call_target="tpu_custom_call" | custom-call | flops 5120 | bytes 5120 | tf_op jit(solution)/shard_map/second_step/pallas_call | solution.py:179
  29.2 2.0 %collective-permute-done.5.part_ref = f32[1920,128]{1,0:T(8,128)S(1)} collective-permute-done((f32[1920,128]{1,0:T(8,128)S(1)}, f32[1920,128]{1,0:T(8,128)S(1)}, u32[]{:S(2)}, u32[]{:S(2)}) %collective-permute-start.5) | collective-permute-done | bytes 983072 | tf_op jit(solution)/shard_map/ppermute | solution.py:270
  31.3 0.7 add_beyond.2.into_ref
  31.9 2.8 %collective-permute-done.6.part_ref = f32[640,128]{1,0:T(8,128)S(1)} collective-permute-done((f32[640,128]{1,0:T(8,128)S(1)}, f32[640,128]{1,0:T(8,128)S(1)}, u32[]{:S(2)}, u32[]{:S(2)}) %collective-permute-start.6) | collective-permute-done | bytes 327712 | tf_op jit(solution)/shard_map/ppermute | solution.py:270
  34.8 0.0 copy-start.1
  34.8 0.0 copy-start.2
  34.8 0.6 add_beyond.3
  35.4 0.0 copy-start
  35.4 53.8 %all_to_all.5 = f32[256,1,1280]{2,1,0:T(1,128)S(1)} all-to-all(f32[256,1,1280]{2,1,0:T(1,128)S(1)} %bitcast.19), channel_id=1, replica_groups=mesh['side'=2,'brick'=128] {'side','brick'}, dimensions={0} | all-to-all | bytes 2621440 | tf_op jit(solution)/shard_map/all_to_all | solution.py:294
  89.2 0.0 copy-done.1
  89.2 0.0 copy-done.2
  89.2 0.0 copy-done
  89.2 3.2 %accumulate.1 = (f32[10,256,128]{2,1,0:T(8,128)}, f32[10,256,128]{2,1,0:T(8,128)}, f32[16,256,128]{2,1,0:T(8,128)}, f32[16,256,128]{2,1,0:T(8,128)}) custom-call(f32[2,1280,128]{2,1,0:T(8,128)S(1)} %bitcast.20, f32[10,256,128]{2,1,0:T(8,128)S(1)} %bitcast.22, f32[10,256,128]{2,1,0:T(8,128)S(1)} %bitcast.23, f32[16,256,128]{2,1,0:T(8,128)S(1)} %bitcast.21), custom_call_target="tpu_custom_call" | custom-call | flops 13107200 | bytes 13631488 | tf_op jit(solution)/shard_map/accumulate/pallas_call | solution.py:238
Async XLA Ops:
  0.6 20.1 %collective-permute-start.2 = (f32[5,256,256]{2,1,0:T(8,128)}, f32[5,256,256]{2,1,0:T(8,128)S(1)}, u32[]{:S(2)}, u32[]{:S(2)}) collective-permute-start(f32[5,256,256]{2,1,0:T(8,128)} %bitcast.25), channel_id=1, source_target_pairs={{1,2},{3,4},{5,6},{7,8},{9,10},{11,12},{13,14},{15,16},{17,18},{19... | collective-permute-start | bytes 3932168 | tf_op jit(solution)/shard_map/ppermute | solution.py:270
  5.2 3.1 %copy-start.4 = (f32[8]{0:T(128)S(1)}, f32[8]{0:T(128)}, u32[]{:S(2)}) copy-start(f32[8]{0:T(128)} %param.10) | copy-start | bytes 100
  5.2 3.1 %copy-start.5 = (f32[8]{0:T(128)S(1)}, f32[8]{0:T(128)}, u32[]{:S(2)}) copy-start(f32[8]{0:T(128)} %param.9) | copy-start | bytes 100
  6.5 3.4 %collective-permute-start = (f32[3,256,256]{2,1,0:T(8,128)S(1)}, f32[3,256,256]{2,1,0:T(8,128)S(1)}, u32[]{:S(2)}, u32[]{:S(2)}) collective-permute-start(f32[3,256,256]{2,1,0:T(8,128)S(1)} %slice_bitcast_fusion.refs_0_), channel_id=1, source_target_pairs={{0,1},{1,0},{2,3},{3,2},{4,5},{5,4},{6,7},{7,6},{8,9},{9,8},{10,11... | collective-permute-start | bytes 2359304 | tf_op jit(solution)/shard_map/ppermute | solution.py:270
  7.7 2.2 %collective-permute-start.1 = (f32[2,256,256]{2,1,0:T(8,128)S(1)}, f32[2,256,256]{2,1,0:T(8,128)}, u32[]{:S(2)}, u32[]{:S(2)}) collective-permute-start(f32[2,256,256]{2,1,0:T(8,128)S(1)} %slice_bitcast_fusion.1.refs_2_.refs_1_), channel_id=1, source_target_pairs={{0,1},{1,0},{2,3},{3,2},{4,5},{5,4},{6,7},{7,6},{8,9},{9,8},{10,11... | collective-permute-start | bytes 1572872 | tf_op jit(solution)/shard_map/ppermute | solution.py:270
  9.9 1.0 %copy-start.3 = (f32[1,256,256]{2,1,0:T(8,128)S(1)}, f32[1,256,256]{2,1,0:T(8,128)}, u32[]{:S(2)}) copy-start(f32[1,256,256]{2,1,0:T(8,128)} %param.8) | copy-start | bytes 786436
  13.3 18.0 %collective-permute-start.5 = (f32[1920,128]{1,0:T(8,128)S(1)}, f32[1920,128]{1,0:T(8,128)S(1)}, u32[]{:S(2)}, u32[]{:S(2)}) collective-permute-start(f32[1920,128]{1,0:T(8,128)S(1)} %get-tuple-element.18), channel_id=1, source_target_pairs={{1,2},{3,4},{5,6},{7,8},{9,10},{11,12},{13,14},{15,16},{17,18},{19... | collective-permute-start | bytes 2949128 | tf_op jit(solution)/shard_map/ppermute | solution.py:270
  21.5 5.9 %collective-permute-start.3 = (f32[3,256,256]{2,1,0:T(8,128)S(1)}, f32[3,256,256]{2,1,0:T(8,128)S(1)}, u32[]{:S(2)}, u32[]{:S(2)}) collective-permute-start(f32[3,256,256]{2,1,0:T(8,128)S(1)} %get-tuple-element.16.refs_0_), channel_id=1, source_target_pairs={{0,1},{1,0},{2,3},{3,2},{4,5},{5,4},{6,7},{7,6},{8,9},{9,8},{10,11... | collective-permute-start | bytes 2359304 | tf_op jit(solution)/shard_map/ppermute | solution.py:270
  21.6 5.8 %collective-permute-start.4 = (f32[2,256,256]{2,1,0:T(8,128)S(1)}, f32[2,256,256]{2,1,0:T(8,128)S(1)}, u32[]{:S(2)}, u32[]{:S(2)}) collective-permute-start(f32[2,256,256]{2,1,0:T(8,128)S(1)} %get-tuple-element.17.refs_2_), channel_id=1, source_target_pairs={{0,1},{1,0},{2,3},{3,2},{4,5},{5,4},{6,7},{7,6},{8,9},{9,8},{10,11... | collective-permute-start | bytes 1572872 | tf_op jit(solution)/shard_map/ppermute | solution.py:270
  22.1 12.7 %collective-permute-start.6 = (f32[640,128]{1,0:T(8,128)S(1)}, f32[640,128]{1,0:T(8,128)S(1)}, u32[]{:S(2)}, u32[]{:S(2)}) collective-permute-start(f32[640,128]{1,0:T(8,128)S(1)} %get-tuple-element.19), channel_id=1, source_target_pairs={{1,2},{3,4},{5,6},{7,8},{9,10},{11,12},{13,14},{15,16},{17,18},{19... | collective-permute-start | bytes 983048 | tf_op jit(solution)/shard_map/ppermute | solution.py:270
  34.8 54.4 %copy-start.1 = (f32[10,128,1,256]{3,2,1,0:T(1,128)S(1)}, f32[10,128,1,256]{3,2,1,0:T(1,128)}, u32[]{:S(2)}) copy-start(f32[10,128,1,256]{3,2,1,0:T(1,128)} %param.11) | copy-start | bytes 3932164
  34.8 54.4 %copy-start.2 = (f32[10,128,1,256]{3,2,1,0:T(1,128)S(1)}, f32[10,128,1,256]{3,2,1,0:T(1,128)}, u32[]{:S(2)}) copy-start(f32[10,128,1,256]{3,2,1,0:T(1,128)} %param.12) | copy-start | bytes 3932164
  35.4 53.8 %copy-start = (f32[16,128,1,256]{3,2,1,0:T(1,128)S(1)}, f32[16,128,1,256]{3,2,1,0:T(1,128)}, u32[]{:S(2)}) copy-start(f32[16,128,1,256]{3,2,1,0:T(1,128)} %param.13) | copy-start | bytes 6291460

commit v5 on v4

--- a/solution.py
+++ b/solution.py
@@ -13,7 +13,6 @@
 UPPER = np.asarray((0.12, 0.12, 0.12, 0.06, 0.2, 1.0, 1.5, 0.1), np.float32)
 WIDTH = UPPER - LOWER
 ROWS = 64
-LAST = 64
 
 
 def weights_of(table_ref, m):
@@ -71,7 +70,7 @@
 
 
 def send_kernel(table_ref, source_ref, *refs):
-    pieces, (out_ref, last_ref, partial_ref, source_copy_ref) = refs[:-4], refs[-4:]
+    pieces, (out_ref, partial_ref, source_copy_ref) = refs[:-3], refs[-3:]
     count, ny, nz = partial_ref.shape
     for r in range(0, ny, ROWS):
         source_copy_ref[r : r + ROWS, :] = source_ref[r : r + ROWS, :]
@@ -85,10 +84,7 @@
             for r in range(0, ny, ROWS):
                 rows = slice(r, r + ROWS)
                 rest = near_w * near_ref[j, rows, :] + amplitude * source_ref[rows, :]
-                if r < ny - LAST:
-                    store_strips(out_ref, m, count, r, near_w * rest)
-                else:
-                    store_strips(last_ref, m, count, r - (ny - LAST), near_w * rest)
+                store_strips(out_ref, m, count, r, near_w * rest)
 
             def store(r, new):
                 partial_ref[m, r : r + ROWS, :] = new
@@ -162,30 +158,28 @@
         first += own_ref.shape[0]
 
 
-def add_kernel(first, table_ref, into_ref, part_ref, out_ref):
+def add_kernel(first_ref, second_ref, out_ref):
     rows = 320
 
     def some_rows(i, carry):
-        start = pl.multiple_of(i * rows, rows)
-        at = pl.ds(first + start, rows)
-        out_ref[at, :] = into_ref[at, :] + part_ref[pl.ds(start, rows), :]
+        at = pl.ds(pl.multiple_of(i * rows, rows), rows)
+        out_ref[at, :] = first_ref[at, :] + second_ref[at, :]
         return carry
 
-    lax.fori_loop(0, part_ref.shape[0] // rows, some_rows, 0)
-
-
-def call(kernel, name, table, arrays, out_shapes, cells, aliases={}):
+    lax.fori_loop(0, out_ref.shape[0] // rows, some_rows, 0)
+
+
+def call(kernel, name, scalars, arrays, out_shapes, cells):
     whole = pl.BlockSpec(memory_space=pltpu.VMEM)
     return pl.pallas_call(
         kernel,
-        in_specs=[pl.BlockSpec(memory_space=pltpu.SMEM)] + [whole] * len(arrays),
+        in_specs=[pl.BlockSpec(memory_space=pltpu.SMEM)] * len(scalars) + [whole] * len(arrays),
         out_specs=[whole] * len(out_shapes),
         out_shape=[jax.ShapeDtypeStruct(shape, jnp.float32) for shape in out_shapes],
-        input_output_aliases=aliases,
         compiler_params=pltpu.CompilerParams(vmem_limit_bytes=32 * 1024 * 1024),
         cost_estimate=pl.CostEstimate(flops=cells // 64, bytes_accessed=cells // 64, transcendentals=0),
         name=name,
-    )(table, *arrays)
+    )(*scalars, *arrays)
 
 
 def accumulate_kernel(count, xb, gathered, means_ref, squares_ref, cross_ref, *refs):
@@ -274,23 +268,17 @@
     flat_shape = (raw.size // 128, 128)
     far = send(raw, far_route)
     pairs = [x for piece in halves for x in (piece, send(piece, near_route))]
-    cut = (ny - LAST) * count * (nz // 128)
-    *beyond, partial, source = call(
-        send_kernel, "send_planes", table, (source, *pairs),
-        ((cut, 128), (raw.size // 128 - cut, 128), raw.shape, source.shape), raw.size,
-    )
-    beyond = [send(part, far_route) for part in beyond]
+    beyond, partial, source = call(
+        send_kernel, "send_planes", (table,), (source, *pairs), (flat_shape, raw.shape, source.shape), raw.size
+    )
+    beyond = send(beyond, far_route)
     ahead = call(
-        first_kernel, "first_step", table, (partial, far), [piece.shape for piece in halves], raw.size
+        first_kernel, "first_step", (table,), (partial, far), [piece.shape for piece in halves], raw.size
     )
     pairs = [x for piece in ahead for x in (piece, send(piece, near_route))]
-    (far_part,) = call(far_kernel, "far_step", table, (far, *halves), (raw.shape,), raw.size)
-    (mine,) = call(second_kernel, "second_step", table, (source, far_part, *pairs), (flat_shape,), raw.size)
-    for start, part in zip((0, cut), beyond):
-        (mine,) = call(
-            functools.partial(add_kernel, start), "add_beyond", table, (mine, part), (flat_shape,), part.size // 8,
-            aliases={1: 0},
-        )
+    (far_part,) = call(far_kernel, "far_step", (table,), (far, *halves), (raw.shape,), raw.size)
+    (mine,) = call(second_kernel, "second_step", (table,), (source, far_part, *pairs), (flat_shape,), raw.size)
+    (mine,) = call(add_kernel, "add_beyond", (), (mine, beyond), (flat_shape,), raw.size // 8)
     strips = lax.all_to_all(
         mine.reshape(256, 1, count * 256), ("side", "brick"), split_axis=0, concat_axis=0, tiled=True
     )

time: 92.7 us -> 92.2 us (level)
  waiting for transfers between devices: 10.4 us -> 14.7 us
  starting transfers between devices: 13 us -> 9.32 us
  Pallas kernels: 11.1 us -> 9.95 us
    ppermute x7 -> x6, waiting for transfers between devices: 10.4 us -> 14.7 us  [body(): send = lambda x, route: lax.ppermute(x, 'brick', route)]
    ppermute x7 -> x6, starting transfers between devices: 13 us -> 9.32 us  [body(): send = lambda x, route: lax.ppermute(x, 'brick', route)]
    pallas_call x6 -> x5, Pallas kernels: 7.88 us -> 6.78 us  [call(): pl.pallas_call(kernel, in_specs=[pl.BlockSpec(memory_space=pltpu.SMEM)] *...]
  transfers between devices with their start and end apart: 7 -> 6, of which waited for: 4 -> 4; matrix products, arithmetic and copies ran while one was open for 3% -> 3% of each run, Pallas kernels for 8% -> 7%
where the time goes in v5:
time: 92.2 us; the launch traced here: 91.9 us
  blocking collectives  53.8 us (58%)
  waiting for transfers between devices  14.7 us (16%)
  Pallas kernels  9.95 us (11%)
  starting transfers between devices  9.32 us (10%)
  local copies, waits for them, and re-layouts  3.27 us (4%)
    all_to_all x1, blocking collectives, body(): lax.all_to_all(mine.reshape(256, 1, count * 256), ('side', 'brick'), spli...  53.8 us
    ppermute x6, waiting for transfers between devices, body(): send = lambda x, route: lax.ppermute(x, 'brick', route)  14.7 us
    ppermute x6, starting transfers between devices, body(): send = lambda x, route: lax.ppermute(x, 'brick', route)  9.32 us
    pallas_call x5, Pallas kernels, call(): pl.pallas_call(kernel, in_specs=[pl.BlockSpec(memory_space=pltpu.SMEM)] *...  6.78 us
    pallas_call x1, Pallas kernels, accumulate(): pl.pallas_call(functools.partial(accumulate_kernel, count, xb), in_specs=...  3.17 us
    slice x2, local copies, waits for them, and re-layouts, body(): halves = (raw[:half], raw[half:])  2.29 us
  transfers between devices with their start and end apart: 6, of which 4 were waited for; matrix products, arithmetic and copies ran while one was open for 3% of the time, Pallas kernels for 7%

profile of v5, /device:TPU:1, one launch (start us, length us, event | category | flops | bytes accessed | tf_op | source)
XLA Modules:
  0.0 91.9 jit_solution(8764917960859517551)
XLA Ops:
  0.6 4.6 %collective-permute-start.2 = (f32[5,256,256]{2,1,0:T(8,128)}, f32[5,256,256]{2,1,0:T(8,128)S(1)}, u32[]{:S(2)}, u32[]{:S(2)}) collective-permute-start(f32[5,256,256]{2,1,0:T(8,128)} %bitcast.25), channel_id=1, source_target_pairs={{1,2},{3,4},{5,6},{7,8},{9,10},{11,12},{13,14},{15,16},{17,18},{19... | collective-permute-start | bytes 3932168 | tf_op jit(solution)/shard_map/ppermute | solution.py:264
  5.2 0.0 copy-start.4
  5.2 0.0 copy-start.5
  5.3 1.2 %slice_bitcast_fusion.refs_0_ = f32[3,256,256]{2,1,0:T(8,128)S(1)} fusion(f32[5,1,256,256]{3,2,0,1:T(8,128)} %bitcast.26), kind=kLoop, calls=%fused_computation | loop fusion | bytes 1572864 | tf_op jit(solution)/shard_map/slice | solution.py:267
  6.5 0.1 collective-permute-start
  6.6 1.1 %slice_bitcast_fusion.1.refs_2_.refs_1_ = f32[2,256,256]{2,1,0:T(8,128)S(1)} fusion(f32[5,1,256,256]{3,2,0,1:T(8,128)} %bitcast.27), kind=kLoop, calls=%fused_computation.1 | loop fusion | bytes 1048576 | tf_op jit(solution)/shard_map/slice | solution.py:267
  7.7 0.6 collective-permute-start.1
  8.2 0.1 add_convert_fusion
  8.3 0.0 copy-done.4
  8.3 0.0 copy-done.5
  8.3 0.1 pad_maximum_fusion.table_ref
  8.4 1.5 %collective-permute-done.1.refs_3_ = f32[2,256,256]{2,1,0:T(8,128)} collective-permute-done((f32[2,256,256]{2,1,0:T(8,128)S(1)}, f32[2,256,256]{2,1,0:T(8,128)}, u32[]{:S(2)}, u32[]{:S(2)}) %collective-permute-start.1) | collective-permute-done | bytes 524320 | tf_op jit(solution)/shard_map/ppermute | solution.py:264
  9.9 0.0 collective-permute-done.refs_1_
  9.9 0.0 copy-start.3
  9.9 0.9 %copy-done.3 = f32[1,256,256]{2,1,0:T(8,128)S(1)} copy-done((f32[1,256,256]{2,1,0:T(8,128)S(1)}, f32[1,256,256]{2,1,0:T(8,128)}, u32[]{:S(2)}) %copy-start.3) | copy-done | bytes 262168
  10.9 2.4 %send_planes.1 = (f32[2560,128]{1,0:T(8,128)S(1)}, f32[5,256,256]{2,1,0:T(8,128)S(1)}, f32[256,256]{1,0:T(8,128)S(1)}) custom-call(f32[19]{0:T(128)S(1)} %pad_maximum_fusion.table_ref, f32[256,256]{1,0:T(8,128)S(1)} %bitcast.24, f32[3,256,256]{2,1,0:T(8,128)S(1)} %slice_bitcast_fusion.refs_0_, f32[3,256,256]{2,1,0:T(8,128)S(1)} %collective-permute-done.refs_1_, ...), custom_call_target="tpu_custom_call" | custom-call | flops 5120 | bytes 5120 | tf_op jit(solution)/shard_map/send_planes/pallas_call | solution.py:174
  13.3 3.5 %collective-permute-start.5 = (f32[2560,128]{1,0:T(8,128)S(1)}, f32[2560,128]{1,0:T(8,128)S(1)}, u32[]{:S(2)}, u32[]{:S(2)}) collective-permute-start(f32[2560,128]{1,0:T(8,128)S(1)} %get-tuple-element.17), channel_id=1, source_target_pairs={{1,2},{3,4},{5,6},{7,8},{9,10},{11,12},{13,14},{15,16},{17,18},{19... | collective-permute-start | bytes 3932168 | tf_op jit(solution)/shard_map/ppermute | solution.py:264
  16.7 4.0 %collective-permute-done.2.raw_far_ref.far_ref = f32[5,256,256]{2,1,0:T(8,128)S(1)} collective-permute-done((f32[5,256,256]{2,1,0:T(8,128)}, f32[5,256,256]{2,1,0:T(8,128)S(1)}, u32[]{:S(2)}, u32[]{:S(2)}) %collective-permute-start.2) | collective-permute-done | bytes 1310752 | tf_op jit(solution)/shard_map/ppermute | solution.py:264
  20.7 0.7 first_step.1
  21.5 0.1 collective-permute-start.3
  21.6 0.5 collective-permute-start.4
  22.1 1.7 %far_step.1.far_part_ref = f32[5,256,256]{2,1,0:T(8,128)S(1)} custom-call(f32[19]{0:T(128)S(1)} %pad_maximum_fusion.table_ref, f32[5,256,256]{2,1,0:T(8,128)S(1)} %collective-permute-done.2.raw_far_ref.far_ref, f32[3,256,256]{2,1,0:T(8,128)S(1)} %slice_bitcast_fusion.refs_0_, f32[2,256,256]{2,1,0:T(8,128)S(1)} %slice_bitcast_fusion.1.refs_2_.refs_1_), custom_call_target="tpu_custom_call" | custom-call | flops 5120 | bytes 5120 | tf_op jit(solution)/shard_map/far_step/pallas_call | solution.py:174
  23.7 0.8 collective-permute-done.4.refs_3_
  24.6 0.0 collective-permute-done.3.refs_1_
  24.6 1.8 %second_step.1.first_ref = f32[2560,128]{1,0:T(8,128)S(1)} custom-call(f32[19]{0:T(128)S(1)} %pad_maximum_fusion.table_ref, f32[256,256]{1,0:T(8,128)S(1)} %get-tuple-element.13.source_ref, f32[5,256,256]{2,1,0:T(8,128)S(1)} %far_step.1.far_part_ref, f32[3,256,256]{2,1,0:T(8,128)S(1)} %get-tuple-element.15.refs_0_, ...), custom_call_target="tpu_custom_call" | custom-call | flops 5120 | bytes 5120 | tf_op jit(solution)/shard_map/second_step/pallas_call | solution.py:174
  26.4 8.4 %collective-permute-done.5.second_ref = f32[2560,128]{1,0:T(8,128)S(1)} collective-permute-done((f32[2560,128]{1,0:T(8,128)S(1)}, f32[2560,128]{1,0:T(8,128)S(1)}, u32[]{:S(2)}, u32[]{:S(2)}) %collective-permute-start.5) | collective-permute-done | bytes 1310752 | tf_op jit(solution)/shard_map/ppermute | solution.py:264
  34.8 0.0 copy-start.1
  34.8 0.0 copy-start.2
  34.8 0.2 add_beyond.1
  34.9 0.0 copy-start
  34.9 53.8 %all_to_all.5 = f32[256,1,1280]{2,1,0:T(1,128)S(1)} all-to-all(f32[256,1,1280]{2,1,0:T(1,128)S(1)} %bitcast.20), channel_id=1, replica_groups=mesh['side'=2,'brick'=128] {'side','brick'}, dimensions={0} | all-to-all | bytes 2621440 | tf_op jit(solution)/shard_map/all_to_all | solution.py:282
  88.7 0.0 copy-done.1
  88.7 0.0 copy-done.2
  88.7 0.0 copy-done
  88.7 3.2 %accumulate.1 = (f32[10,256,128]{2,1,0:T(8,128)}, f32[10,256,128]{2,1,0:T(8,128)}, f32[16,256,128]{2,1,0:T(8,128)}, f32[16,256,128]{2,1,0:T(8,128)}) custom-call(f32[2,1280,128]{2,1,0:T(8,128)S(1)} %bitcast.19, f32[10,256,128]{2,1,0:T(8,128)S(1)} %bitcast.22, f32[10,256,128]{2,1,0:T(8,128)S(1)} %bitcast.23, f32[16,256,128]{2,1,0:T(8,128)S(1)} %bitcast.21), custom_call_target="tpu_custom_call" | custom-call | flops 13107200 | bytes 13631488 | tf_op jit(solution)/shard_map/accumulate/pallas_call | solution.py:232
Async XLA Ops:
  0.6 20.1 %collective-permute-start.2 = (f32[5,256,256]{2,1,0:T(8,128)}, f32[5,256,256]{2,1,0:T(8,128)S(1)}, u32[]{:S(2)}, u32[]{:S(2)}) collective-permute-start(f32[5,256,256]{2,1,0:T(8,128)} %bitcast.25), channel_id=1, source_target_pairs={{1,2},{3,4},{5,6},{7,8},{9,10},{11,12},{13,14},{15,16},{17,18},{19... | collective-permute-start | bytes 3932168 | tf_op jit(solution)/shard_map/ppermute | solution.py:264
  5.2 3.1 %copy-start.4 = (f32[8]{0:T(128)S(1)}, f32[8]{0:T(128)}, u32[]{:S(2)}) copy-start(f32[8]{0:T(128)} %param.10) | copy-start | bytes 100
  5.2 3.1 %copy-start.5 = (f32[8]{0:T(128)S(1)}, f32[8]{0:T(128)}, u32[]{:S(2)}) copy-start(f32[8]{0:T(128)} %param.9) | copy-start | bytes 100
  6.5 3.4 %collective-permute-start = (f32[3,256,256]{2,1,0:T(8,128)S(1)}, f32[3,256,256]{2,1,0:T(8,128)S(1)}, u32[]{:S(2)}, u32[]{:S(2)}) collective-permute-start(f32[3,256,256]{2,1,0:T(8,128)S(1)} %slice_bitcast_fusion.refs_0_), channel_id=1, source_target_pairs={{0,1},{1,0},{2,3},{3,2},{4,5},{5,4},{6,7},{7,6},{8,9},{9,8},{10,11... | collective-permute-start | bytes 2359304 | tf_op jit(solution)/shard_map/ppermute | solution.py:264
  7.7 2.2 %collective-permute-start.1 = (f32[2,256,256]{2,1,0:T(8,128)S(1)}, f32[2,256,256]{2,1,0:T(8,128)}, u32[]{:S(2)}, u32[]{:S(2)}) collective-permute-start(f32[2,256,256]{2,1,0:T(8,128)S(1)} %slice_bitcast_fusion.1.refs_2_.refs_1_), channel_id=1, source_target_pairs={{0,1},{1,0},{2,3},{3,2},{4,5},{5,4},{6,7},{7,6},{8,9},{9,8},{10,11... | collective-permute-start | bytes 1572872 | tf_op jit(solution)/shard_map/ppermute | solution.py:264
  9.9 1.0 %copy-start.3 = (f32[1,256,256]{2,1,0:T(8,128)S(1)}, f32[1,256,256]{2,1,0:T(8,128)}, u32[]{:S(2)}) copy-start(f32[1,256,256]{2,1,0:T(8,128)} %param.8) | copy-start | bytes 786436
  13.3 21.5 %collective-permute-start.5 = (f32[2560,128]{1,0:T(8,128)S(1)}, f32[2560,128]{1,0:T(8,128)S(1)}, u32[]{:S(2)}, u32[]{:S(2)}) collective-permute-start(f32[2560,128]{1,0:T(8,128)S(1)} %get-tuple-element.17), channel_id=1, source_target_pairs={{1,2},{3,4},{5,6},{7,8},{9,10},{11,12},{13,14},{15,16},{17,18},{19... | collective-permute-start | bytes 3932168 | tf_op jit(solution)/shard_map/ppermute | solution.py:264
  21.5 3.1 %collective-permute-start.3 = (f32[3,256,256]{2,1,0:T(8,128)S(1)}, f32[3,256,256]{2,1,0:T(8,128)S(1)}, u32[]{:S(2)}, u32[]{:S(2)}) collective-permute-start(f32[3,256,256]{2,1,0:T(8,128)S(1)} %get-tuple-element.15.refs_0_), channel_id=1, source_target_pairs={{0,1},{1,0},{2,3},{3,2},{4,5},{5,4},{6,7},{7,6},{8,9},{9,8},{10,11... | collective-permute-start | bytes 2359304 | tf_op jit(solution)/shard_map/ppermute | solution.py:264
  21.6 3.0 %collective-permute-start.4 = (f32[2,256,256]{2,1,0:T(8,128)S(1)}, f32[2,256,256]{2,1,0:T(8,128)S(1)}, u32[]{:S(2)}, u32[]{:S(2)}) collective-permute-start(f32[2,256,256]{2,1,0:T(8,128)S(1)} %get-tuple-element.16.refs_2_), channel_id=1, source_target_pairs={{0,1},{1,0},{2,3},{3,2},{4,5},{5,4},{6,7},{7,6},{8,9},{9,8},{10,11... | collective-permute-start | bytes 1572872 | tf_op jit(solution)/shard_map/ppermute | solution.py:264
  34.8 54.0 %copy-start.1 = (f32[10,128,1,256]{3,2,1,0:T(1,128)S(1)}, f32[10,128,1,256]{3,2,1,0:T(1,128)}, u32[]{:S(2)}) copy-start(f32[10,128,1,256]{3,2,1,0:T(1,128)} %param.11) | copy-start | bytes 3932164
  34.8 54.0 %copy-start.2 = (f32[10,128,1,256]{3,2,1,0:T(1,128)S(1)}, f32[10,128,1,256]{3,2,1,0:T(1,128)}, u32[]{:S(2)}) copy-start(f32[10,128,1,256]{3,2,1,0:T(1,128)} %param.12) | copy-start | bytes 3932164
  34.9 53.8 %copy-start = (f32[16,128,1,256]{3,2,1,0:T(1,128)S(1)}, f32[16,128,1,256]{3,2,1,0:T(1,128)}, u32[]{:S(2)}) copy-start(f32[16,128,1,256]{3,2,1,0:T(1,128)} %param.13) | copy-start | bytes 6291460

commit v6 on v5

--- a/solution.py
+++ b/solution.py
@@ -182,21 +182,22 @@
     )(*scalars, *arrays)
 
 
-def accumulate_kernel(count, xb, gathered, means_ref, squares_ref, cross_ref, *refs):
+def accumulate_kernel(count, blocks_of, gathered, means_ref, squares_ref, cross_ref, *refs):
     outs, blocks, (held, copied) = refs[:4], refs[4:8], refs[8:]
     new_means_ref, new_squares_ref, new_cross_ref, maps_ref = blocks
     copies = []
-    for i in range(128 // xb):
-        rows = pl.ds(i * 2 * xb, 2 * xb)
+    start = 0
+    for i, xb in enumerate(blocks_of):
+        rows = pl.ds(2 * start, 2 * xb)
         for s in range(2):
             for m in range(count):
                 for h in range(2):
                     held[s * count + m, pl.ds(h, xb, stride=2), :] = gathered[
-                        s, pl.ds(i * (xb * 2 * count) + m * 2 + h, xb, stride=2 * count), :
+                        s, pl.ds(start * 2 * count + m * 2 + h, xb, stride=2 * count), :
                     ]
 
         def moments(m):
-            out, mean = held[m], means_ref[m, rows, :]
+            out, mean = held[m, : 2 * xb, :], means_ref[m, rows, :]
             deviation = out - mean
             new_mean = mean + deviation * (1.0 / (PRIOR + 1))
             after = out - new_mean
@@ -219,23 +220,24 @@
             copy = pltpu.make_async_copy(block.at[:, rows], out.at[:, rows], copied.at[i, j])
             copy.start()
             copies.append(copy)
+        start += xb
     for copy in copies:
         copy.wait()
 
 
 def accumulate(gathered, count, means, squares, cross):
-    xb = 32
-    nx = 128
+    blocks_of = (8, 16, 40, 64)
+    nx = sum(blocks_of)
     whole = pl.BlockSpec(memory_space=pltpu.VMEM)
     shape = lambda lead: (lead, 2 * nx, 128)
     leads = (10, 10, 16, 16)
     return pl.pallas_call(
-        functools.partial(accumulate_kernel, count, xb),
+        functools.partial(accumulate_kernel, count, blocks_of),
         in_specs=[whole] * 4,
         out_specs=[pl.BlockSpec(memory_space=pl.ANY)] * 4,
         out_shape=[jax.ShapeDtypeStruct(shape(lead), jnp.float32) for lead in leads],
         scratch_shapes=[pltpu.VMEM(shape(lead), jnp.float32) for lead in leads]
-        + [pltpu.VMEM((10, 2 * xb, 128), jnp.float32), pltpu.SemaphoreType.DMA((nx // xb, 4))],
+        + [pltpu.VMEM((10, 2 * max(blocks_of), 128), jnp.float32), pltpu.SemaphoreType.DMA((len(blocks_of), 4))],
         compiler_params=pltpu.CompilerParams(vmem_limit_bytes=32 * 1024 * 1024),
         cost_estimate=pl.CostEstimate(
             flops=40 * 10 * nx * 256, bytes_accessed=13 * 1024 * 1024, transcendentals=16 * nx * 256

time: 92.2 us -> 92.1 us (level)
  no operation moved by 1% of the time
where the time goes in v6:
time: 92.1 us; the launch traced here: 91.8 us
  blocking collectives  53.8 us (58%)
  waiting for transfers between devices  14.7 us (16%)
  Pallas kernels  9.82 us (11%)
  starting transfers between devices  9.32 us (10%)
  local copies, waits for them, and re-layouts  3.27 us (4%)
    all_to_all x1, blocking collectives, body(): lax.all_to_all(mine.reshape(256, 1, count * 256), ('side', 'brick'), spli...  53.8 us
    ppermute x6, waiting for transfers between devices, body(): send = lambda x, route: lax.ppermute(x, 'brick', route)  14.7 us
    ppermute x6, starting transfers between devices, body(): send = lambda x, route: lax.ppermute(x, 'brick', route)  9.32 us
    pallas_call x5, Pallas kernels, call(): pl.pallas_call(kernel, in_specs=[pl.BlockSpec(memory_space=pltpu.SMEM)] *...  6.78 us
    pallas_call x1, Pallas kernels, accumulate(): pl.pallas_call(functools.partial(accumulate_kernel, count, blocks_of), in...  3.04 us
    slice x2, local copies, waits for them, and re-layouts, body(): halves = (raw[:half], raw[half:])  2.29 us
  transfers between devices with their start and end apart: 6, of which 4 were waited for; matrix products, arithmetic and copies ran while one was open for 3% of the time, Pallas kernels for 7%

profile of v6, /device:TPU:1, one launch (start us, length us, event | category | flops | bytes accessed | tf_op | source)
XLA Modules:
  0.0 91.8 jit_solution(9577994819054940940)
XLA Ops:
  0.6 4.6 %collective-permute-start.2 = (f32[5,256,256]{2,1,0:T(8,128)}, f32[5,256,256]{2,1,0:T(8,128)S(1)}, u32[]{:S(2)}, u32[]{:S(2)}) collective-permute-start(f32[5,256,256]{2,1,0:T(8,128)} %bitcast.25), channel_id=1, source_target_pairs={{1,2},{3,4},{5,6},{7,8},{9,10},{11,12},{13,14},{15,16},{17,18},{19... | collective-permute-start | bytes 3932168 | tf_op jit(solution)/shard_map/ppermute | solution.py:266
  5.2 0.0 copy-start.4
  5.2 0.0 copy-start.5
  5.3 1.2 %slice_bitcast_fusion.refs_0_ = f32[3,256,256]{2,1,0:T(8,128)S(1)} fusion(f32[5,1,256,256]{3,2,0,1:T(8,128)} %bitcast.26), kind=kLoop, calls=%fused_computation | loop fusion | bytes 1572864 | tf_op jit(solution)/shard_map/slice | solution.py:269
  6.5 0.1 collective-permute-start
  6.6 1.1 %slice_bitcast_fusion.1.refs_2_.refs_1_ = f32[2,256,256]{2,1,0:T(8,128)S(1)} fusion(f32[5,1,256,256]{3,2,0,1:T(8,128)} %bitcast.27), kind=kLoop, calls=%fused_computation.1 | loop fusion | bytes 1048576 | tf_op jit(solution)/shard_map/slice | solution.py:269
  7.7 0.6 collective-permute-start.1
  8.2 0.1 add_convert_fusion
  8.3 0.0 copy-done.4
  8.3 0.0 copy-done.5
  8.3 0.1 pad_maximum_fusion.table_ref
  8.4 1.5 %collective-permute-done.1.refs_3_ = f32[2,256,256]{2,1,0:T(8,128)} collective-permute-done((f32[2,256,256]{2,1,0:T(8,128)S(1)}, f32[2,256,256]{2,1,0:T(8,128)}, u32[]{:S(2)}, u32[]{:S(2)}) %collective-permute-start.1) | collective-permute-done | bytes 524320 | tf_op jit(solution)/shard_map/ppermute | solution.py:266
  9.9 0.0 collective-permute-done.refs_1_
  9.9 0.0 copy-start.3
  9.9 0.9 %copy-done.3 = f32[1,256,256]{2,1,0:T(8,128)S(1)} copy-done((f32[1,256,256]{2,1,0:T(8,128)S(1)}, f32[1,256,256]{2,1,0:T(8,128)}, u32[]{:S(2)}) %copy-start.3) | copy-done | bytes 262168
  10.9 2.4 %send_planes.1 = (f32[2560,128]{1,0:T(8,128)S(1)}, f32[5,256,256]{2,1,0:T(8,128)S(1)}, f32[256,256]{1,0:T(8,128)S(1)}) custom-call(f32[19]{0:T(128)S(1)} %pad_maximum_fusion.table_ref, f32[256,256]{1,0:T(8,128)S(1)} %bitcast.24, f32[3,256,256]{2,1,0:T(8,128)S(1)} %slice_bitcast_fusion.refs_0_, f32[3,256,256]{2,1,0:T(8,128)S(1)} %collective-permute-done.refs_1_, ...), custom_call_target="tpu_custom_call" | custom-call | flops 5120 | bytes 5120 | tf_op jit(solution)/shard_map/send_planes/pallas_call | solution.py:174
  13.3 3.5 %collective-permute-start.5 = (f32[2560,128]{1,0:T(8,128)S(1)}, f32[2560,128]{1,0:T(8,128)S(1)}, u32[]{:S(2)}, u32[]{:S(2)}) collective-permute-start(f32[2560,128]{1,0:T(8,128)S(1)} %get-tuple-element.17), channel_id=1, source_target_pairs={{1,2},{3,4},{5,6},{7,8},{9,10},{11,12},{13,14},{15,16},{17,18},{19... | collective-permute-start | bytes 3932168 | tf_op jit(solution)/shard_map/ppermute | solution.py:266
  16.7 4.0 %collective-permute-done.2.raw_far_ref.far_ref = f32[5,256,256]{2,1,0:T(8,128)S(1)} collective-permute-done((f32[5,256,256]{2,1,0:T(8,128)}, f32[5,256,256]{2,1,0:T(8,128)S(1)}, u32[]{:S(2)}, u32[]{:S(2)}) %collective-permute-start.2) | collective-permute-done | bytes 1310752 | tf_op jit(solution)/shard_map/ppermute | solution.py:266
  20.7 0.7 first_step.1
  21.5 0.1 collective-permute-start.3
  21.6 0.5 collective-permute-start.4
  22.1 1.7 %far_step.1.far_part_ref = f32[5,256,256]{2,1,0:T(8,128)S(1)} custom-call(f32[19]{0:T(128)S(1)} %pad_maximum_fusion.table_ref, f32[5,256,256]{2,1,0:T(8,128)S(1)} %collective-permute-done.2.raw_far_ref.far_ref, f32[3,256,256]{2,1,0:T(8,128)S(1)} %slice_bitcast_fusion.refs_0_, f32[2,256,256]{2,1,0:T(8,128)S(1)} %slice_bitcast_fusion.1.refs_2_.refs_1_), custom_call_target="tpu_custom_call" | custom-call | flops 5120 | bytes 5120 | tf_op jit(solution)/shard_map/far_step/pallas_call | solution.py:174
  23.7 0.8 collective-permute-done.4.refs_3_
  24.6 0.0 collective-permute-done.3.refs_1_
  24.6 1.8 %second_step.1.first_ref = f32[2560,128]{1,0:T(8,128)S(1)} custom-call(f32[19]{0:T(128)S(1)} %pad_maximum_fusion.table_ref, f32[256,256]{1,0:T(8,128)S(1)} %get-tuple-element.13.source_ref, f32[5,256,256]{2,1,0:T(8,128)S(1)} %far_step.1.far_part_ref, f32[3,256,256]{2,1,0:T(8,128)S(1)} %get-tuple-element.15.refs_0_, ...), custom_call_target="tpu_custom_call" | custom-call | flops 5120 | bytes 5120 | tf_op jit(solution)/shard_map/second_step/pallas_call | solution.py:174
  26.4 8.4 %collective-permute-done.5.second_ref = f32[2560,128]{1,0:T(8,128)S(1)} collective-permute-done((f32[2560,128]{1,0:T(8,128)S(1)}, f32[2560,128]{1,0:T(8,128)S(1)}, u32[]{:S(2)}, u32[]{:S(2)}) %collective-permute-start.5) | collective-permute-done | bytes 1310752 | tf_op jit(solution)/shard_map/ppermute | solution.py:266
  34.8 0.0 copy-start.1
  34.8 0.0 copy-start.2
  34.8 0.2 add_beyond.1
  34.9 0.0 copy-start
  34.9 53.8 %all_to_all.5 = f32[256,1,1280]{2,1,0:T(1,128)S(1)} all-to-all(f32[256,1,1280]{2,1,0:T(1,128)S(1)} %bitcast.20), channel_id=1, replica_groups=mesh['side'=2,'brick'=128] {'side','brick'}, dimensions={0} | all-to-all | bytes 2621440 | tf_op jit(solution)/shard_map/all_to_all | solution.py:284
  88.7 0.0 copy-done.1
  88.7 0.0 copy-done.2
  88.7 0.0 copy-done
  88.7 3.0 %accumulate.1 = (f32[10,256,128]{2,1,0:T(8,128)}, f32[10,256,128]{2,1,0:T(8,128)}, f32[16,256,128]{2,1,0:T(8,128)}, f32[16,256,128]{2,1,0:T(8,128)}) custom-call(f32[2,1280,128]{2,1,0:T(8,128)S(1)} %bitcast.19, f32[10,256,128]{2,1,0:T(8,128)S(1)} %bitcast.22, f32[10,256,128]{2,1,0:T(8,128)S(1)} %bitcast.23, f32[16,256,128]{2,1,0:T(8,128)S(1)} %bitcast.21), custom_call_target="tpu_custom_call" | custom-call | flops 13107200 | bytes 13631488 | tf_op jit(solution)/shard_map/accumulate/pallas_call | solution.py:234
Async XLA Ops:
  0.6 20.1 %collective-permute-start.2 = (f32[5,256,256]{2,1,0:T(8,128)}, f32[5,256,256]{2,1,0:T(8,128)S(1)}, u32[]{:S(2)}, u32[]{:S(2)}) collective-permute-start(f32[5,256,256]{2,1,0:T(8,128)} %bitcast.25), channel_id=1, source_target_pairs={{1,2},{3,4},{5,6},{7,8},{9,10},{11,12},{13,14},{15,16},{17,18},{19... | collective-permute-start | bytes 3932168 | tf_op jit(solution)/shard_map/ppermute | solution.py:266
  5.2 3.1 %copy-start.4 = (f32[8]{0:T(128)S(1)}, f32[8]{0:T(128)}, u32[]{:S(2)}) copy-start(f32[8]{0:T(128)} %param.10) | copy-start | bytes 100
  5.2 3.1 %copy-start.5 = (f32[8]{0:T(128)S(1)}, f32[8]{0:T(128)}, u32[]{:S(2)}) copy-start(f32[8]{0:T(128)} %param.9) | copy-start | bytes 100
  6.5 3.4 %collective-permute-start = (f32[3,256,256]{2,1,0:T(8,128)S(1)}, f32[3,256,256]{2,1,0:T(8,128)S(1)}, u32[]{:S(2)}, u32[]{:S(2)}) collective-permute-start(f32[3,256,256]{2,1,0:T(8,128)S(1)} %slice_bitcast_fusion.refs_0_), channel_id=1, source_target_pairs={{0,1},{1,0},{2,3},{3,2},{4,5},{5,4},{6,7},{7,6},{8,9},{9,8},{10,11... | collective-permute-start | bytes 2359304 | tf_op jit(solution)/shard_map/ppermute | solution.py:266
  7.7 2.2 %collective-permute-start.1 = (f32[2,256,256]{2,1,0:T(8,128)S(1)}, f32[2,256,256]{2,1,0:T(8,128)}, u32[]{:S(2)}, u32[]{:S(2)}) collective-permute-start(f32[2,256,256]{2,1,0:T(8,128)S(1)} %slice_bitcast_fusion.1.refs_2_.refs_1_), channel_id=1, source_target_pairs={{0,1},{1,0},{2,3},{3,2},{4,5},{5,4},{6,7},{7,6},{8,9},{9,8},{10,11... | collective-permute-start | bytes 1572872 | tf_op jit(solution)/shard_map/ppermute | solution.py:266
  9.9 1.0 %copy-start.3 = (f32[1,256,256]{2,1,0:T(8,128)S(1)}, f32[1,256,256]{2,1,0:T(8,128)}, u32[]{:S(2)}) copy-start(f32[1,256,256]{2,1,0:T(8,128)} %param.8) | copy-start | bytes 786436
  13.3 21.5 %collective-permute-start.5 = (f32[2560,128]{1,0:T(8,128)S(1)}, f32[2560,128]{1,0:T(8,128)S(1)}, u32[]{:S(2)}, u32[]{:S(2)}) collective-permute-start(f32[2560,128]{1,0:T(8,128)S(1)} %get-tuple-element.17), channel_id=1, source_target_pairs={{1,2},{3,4},{5,6},{7,8},{9,10},{11,12},{13,14},{15,16},{17,18},{19... | collective-permute-start | bytes 3932168 | tf_op jit(solution)/shard_map/ppermute | solution.py:266
  21.5 3.1 %collective-permute-start.3 = (f32[3,256,256]{2,1,0:T(8,128)S(1)}, f32[3,256,256]{2,1,0:T(8,128)S(1)}, u32[]{:S(2)}, u32[]{:S(2)}) collective-permute-start(f32[3,256,256]{2,1,0:T(8,128)S(1)} %get-tuple-element.15.refs_0_), channel_id=1, source_target_pairs={{0,1},{1,0},{2,3},{3,2},{4,5},{5,4},{6,7},{7,6},{8,9},{9,8},{10,11... | collective-permute-start | bytes 2359304 | tf_op jit(solution)/shard_map/ppermute | solution.py:266
  21.6 3.0 %collective-permute-start.4 = (f32[2,256,256]{2,1,0:T(8,128)S(1)}, f32[2,256,256]{2,1,0:T(8,128)S(1)}, u32[]{:S(2)}, u32[]{:S(2)}) collective-permute-start(f32[2,256,256]{2,1,0:T(8,128)S(1)} %get-tuple-element.16.refs_2_), channel_id=1, source_target_pairs={{0,1},{1,0},{2,3},{3,2},{4,5},{5,4},{6,7},{7,6},{8,9},{9,8},{10,11... | collective-permute-start | bytes 1572872 | tf_op jit(solution)/shard_map/ppermute | solution.py:266
  34.8 54.0 %copy-start.1 = (f32[10,128,1,256]{3,2,1,0:T(1,128)S(1)}, f32[10,128,1,256]{3,2,1,0:T(1,128)}, u32[]{:S(2)}) copy-start(f32[10,128,1,256]{3,2,1,0:T(1,128)} %param.11) | copy-start | bytes 3932164
  34.8 54.0 %copy-start.2 = (f32[10,128,1,256]{3,2,1,0:T(1,128)S(1)}, f32[10,128,1,256]{3,2,1,0:T(1,128)}, u32[]{:S(2)}) copy-start(f32[10,128,1,256]{3,2,1,0:T(1,128)} %param.12) | copy-start | bytes 3932164
  34.9 53.8 %copy-start = (f32[16,128,1,256]{3,2,1,0:T(1,128)S(1)}, f32[16,128,1,256]{3,2,1,0:T(1,128)}, u32[]{:S(2)}) copy-start(f32[16,128,1,256]{3,2,1,0:T(1,128)} %param.13) | copy-start | bytes 6291460

commit v7 on v6

--- a/solution.py
+++ b/solution.py
@@ -226,7 +226,7 @@
 
 
 def accumulate(gathered, count, means, squares, cross):
-    blocks_of = (8, 16, 40, 64)
+    blocks_of = (8, 12, 20, 32, 56)
     nx = sum(blocks_of)
     whole = pl.BlockSpec(memory_space=pltpu.VMEM)
     shape = lambda lead: (lead, 2 * nx, 128)

time: 92.1 us -> 92.1 us (level)
  no operation moved by 1% of the time
where the time goes in v7:
time: 92.1 us; the launch traced here: 91.8 us
  blocking collectives  53.8 us (58%)
  waiting for transfers between devices  14.7 us (16%)
  Pallas kernels  9.83 us (11%)
  starting transfers between devices  9.32 us (10%)
  local copies, waits for them, and re-layouts  3.27 us (4%)
    all_to_all x1, blocking collectives, body(): lax.all_to_all(mine.reshape(256, 1, count * 256), ('side', 'brick'), spli...  53.8 us
    ppermute x6, waiting for transfers between devices, body(): send = lambda x, route: lax.ppermute(x, 'brick', route)  14.7 us
    ppermute x6, starting transfers between devices, body(): send = lambda x, route: lax.ppermute(x, 'brick', route)  9.32 us
    pallas_call x5, Pallas kernels, call(): pl.pallas_call(kernel, in_specs=[pl.BlockSpec(memory_space=pltpu.SMEM)] *...  6.78 us
    pallas_call x1, Pallas kernels, accumulate(): pl.pallas_call(functools.partial(accumulate_kernel, count, blocks_of), in...  3.05 us
    slice x2, local copies, waits for them, and re-layouts, body(): halves = (raw[:half], raw[half:])  2.29 us
  transfers between devices with their start and end apart: 6, of which 4 were waited for; matrix products, arithmetic and copies ran while one was open for 3% of the time, Pallas kernels for 7%

profile of v7, /device:TPU:1, one launch (start us, length us, event | category | flops | bytes accessed | tf_op | source)
XLA Modules:
  0.0 91.8 jit_solution(18333030340564935944)
XLA Ops:
  0.6 4.6 %collective-permute-start.2 = (f32[5,256,256]{2,1,0:T(8,128)}, f32[5,256,256]{2,1,0:T(8,128)S(1)}, u32[]{:S(2)}, u32[]{:S(2)}) collective-permute-start(f32[5,256,256]{2,1,0:T(8,128)} %bitcast.25), channel_id=1, source_target_pairs={{1,2},{3,4},{5,6},{7,8},{9,10},{11,12},{13,14},{15,16},{17,18},{19... | collective-permute-start | bytes 3932168 | tf_op jit(solution)/shard_map/ppermute | solution.py:266
  5.2 0.0 copy-start.4
  5.2 0.0 copy-start.5
  5.3 1.2 %slice_bitcast_fusion.refs_0_ = f32[3,256,256]{2,1,0:T(8,128)S(1)} fusion(f32[5,1,256,256]{3,2,0,1:T(8,128)} %bitcast.26), kind=kLoop, calls=%fused_computation | loop fusion | bytes 1572864 | tf_op jit(solution)/shard_map/slice | solution.py:269
  6.5 0.1 collective-permute-start
  6.6 1.1 %slice_bitcast_fusion.1.refs_2_.refs_1_ = f32[2,256,256]{2,1,0:T(8,128)S(1)} fusion(f32[5,1,256,256]{3,2,0,1:T(8,128)} %bitcast.27), kind=kLoop, calls=%fused_computation.1 | loop fusion | bytes 1048576 | tf_op jit(solution)/shard_map/slice | solution.py:269
  7.7 0.6 collective-permute-start.1
  8.2 0.1 add_convert_fusion
  8.3 0.0 copy-done.4
  8.3 0.0 copy-done.5
  8.3 0.1 pad_maximum_fusion.table_ref
  8.4 1.5 %collective-permute-done.1.refs_3_ = f32[2,256,256]{2,1,0:T(8,128)} collective-permute-done((f32[2,256,256]{2,1,0:T(8,128)S(1)}, f32[2,256,256]{2,1,0:T(8,128)}, u32[]{:S(2)}, u32[]{:S(2)}) %collective-permute-start.1) | collective-permute-done | bytes 524320 | tf_op jit(solution)/shard_map/ppermute | solution.py:266
  9.9 0.0 collective-permute-done.refs_1_
  9.9 0.0 copy-start.3
  9.9 0.9 %copy-done.3 = f32[1,256,256]{2,1,0:T(8,128)S(1)} copy-done((f32[1,256,256]{2,1,0:T(8,128)S(1)}, f32[1,256,256]{2,1,0:T(8,128)}, u32[]{:S(2)}) %copy-start.3) | copy-done | bytes 262168
  10.9 2.4 %send_planes.1 = (f32[2560,128]{1,0:T(8,128)S(1)}, f32[5,256,256]{2,1,0:T(8,128)S(1)}, f32[256,256]{1,0:T(8,128)S(1)}) custom-call(f32[19]{0:T(128)S(1)} %pad_maximum_fusion.table_ref, f32[256,256]{1,0:T(8,128)S(1)} %bitcast.24, f32[3,256,256]{2,1,0:T(8,128)S(1)} %slice_bitcast_fusion.refs_0_, f32[3,256,256]{2,1,0:T(8,128)S(1)} %collective-permute-done.refs_1_, ...), custom_call_target="tpu_custom_call" | custom-call | flops 5120 | bytes 5120 | tf_op jit(solution)/shard_map/send_planes/pallas_call | solution.py:174
  13.3 3.5 %collective-permute-start.5 = (f32[2560,128]{1,0:T(8,128)S(1)}, f32[2560,128]{1,0:T(8,128)S(1)}, u32[]{:S(2)}, u32[]{:S(2)}) collective-permute-start(f32[2560,128]{1,0:T(8,128)S(1)} %get-tuple-element.17), channel_id=1, source_target_pairs={{1,2},{3,4},{5,6},{7,8},{9,10},{11,12},{13,14},{15,16},{17,18},{19... | collective-permute-start | bytes 3932168 | tf_op jit(solution)/shard_map/ppermute | solution.py:266
  16.7 4.0 %collective-permute-done.2.raw_far_ref.far_ref = f32[5,256,256]{2,1,0:T(8,128)S(1)} collective-permute-done((f32[5,256,256]{2,1,0:T(8,128)}, f32[5,256,256]{2,1,0:T(8,128)S(1)}, u32[]{:S(2)}, u32[]{:S(2)}) %collective-permute-start.2) | collective-permute-done | bytes 1310752 | tf_op jit(solution)/shard_map/ppermute | solution.py:266
  20.7 0.7 first_step.1
  21.5 0.1 collective-permute-start.3
  21.6 0.5 collective-permute-start.4
  22.1 1.7 %far_step.1.far_part_ref = f32[5,256,256]{2,1,0:T(8,128)S(1)} custom-call(f32[19]{0:T(128)S(1)} %pad_maximum_fusion.table_ref, f32[5,256,256]{2,1,0:T(8,128)S(1)} %collective-permute-done.2.raw_far_ref.far_ref, f32[3,256,256]{2,1,0:T(8,128)S(1)} %slice_bitcast_fusion.refs_0_, f32[2,256,256]{2,1,0:T(8,128)S(1)} %slice_bitcast_fusion.1.refs_2_.refs_1_), custom_call_target="tpu_custom_call" | custom-call | flops 5120 | bytes 5120 | tf_op jit(solution)/shard_map/far_step/pallas_call | solution.py:174
  23.7 0.8 collective-permute-done.4.refs_3_
  24.6 0.0 collective-permute-done.3.refs_1_
  24.6 1.8 %second_step.1.first_ref = f32[2560,128]{1,0:T(8,128)S(1)} custom-call(f32[19]{0:T(128)S(1)} %pad_maximum_fusion.table_ref, f32[256,256]{1,0:T(8,128)S(1)} %get-tuple-element.13.source_ref, f32[5,256,256]{2,1,0:T(8,128)S(1)} %far_step.1.far_part_ref, f32[3,256,256]{2,1,0:T(8,128)S(1)} %get-tuple-element.15.refs_0_, ...), custom_call_target="tpu_custom_call" | custom-call | flops 5120 | bytes 5120 | tf_op jit(solution)/shard_map/second_step/pallas_call | solution.py:174
  26.4 8.4 %collective-permute-done.5.second_ref = f32[2560,128]{1,0:T(8,128)S(1)} collective-permute-done((f32[2560,128]{1,0:T(8,128)S(1)}, f32[2560,128]{1,0:T(8,128)S(1)}, u32[]{:S(2)}, u32[]{:S(2)}) %collective-permute-start.5) | collective-permute-done | bytes 1310752 | tf_op jit(solution)/shard_map/ppermute | solution.py:266
  34.8 0.0 copy-start.1
  34.8 0.0 copy-start.2
  34.8 0.2 add_beyond.1
  34.9 0.0 copy-start
  34.9 53.8 %all_to_all.5 = f32[256,1,1280]{2,1,0:T(1,128)S(1)} all-to-all(f32[256,1,1280]{2,1,0:T(1,128)S(1)} %bitcast.20), channel_id=1, replica_groups=mesh['side'=2,'brick'=128] {'side','brick'}, dimensions={0} | all-to-all | bytes 2621440 | tf_op jit(solution)/shard_map/all_to_all | solution.py:284
  88.7 0.0 copy-done.1
  88.7 0.0 copy-done.2
  88.7 0.0 copy-done
  88.7 3.1 %accumulate.1 = (f32[10,256,128]{2,1,0:T(8,128)}, f32[10,256,128]{2,1,0:T(8,128)}, f32[16,256,128]{2,1,0:T(8,128)}, f32[16,256,128]{2,1,0:T(8,128)}) custom-call(f32[2,1280,128]{2,1,0:T(8,128)S(1)} %bitcast.19, f32[10,256,128]{2,1,0:T(8,128)S(1)} %bitcast.22, f32[10,256,128]{2,1,0:T(8,128)S(1)} %bitcast.23, f32[16,256,128]{2,1,0:T(8,128)S(1)} %bitcast.21), custom_call_target="tpu_custom_call" | custom-call | flops 13107200 | bytes 13631488 | tf_op jit(solution)/shard_map/accumulate/pallas_call | solution.py:234
Async XLA Ops:
  0.6 20.1 %collective-permute-start.2 = (f32[5,256,256]{2,1,0:T(8,128)}, f32[5,256,256]{2,1,0:T(8,128)S(1)}, u32[]{:S(2)}, u32[]{:S(2)}) collective-permute-start(f32[5,256,256]{2,1,0:T(8,128)} %bitcast.25), channel_id=1, source_target_pairs={{1,2},{3,4},{5,6},{7,8},{9,10},{11,12},{13,14},{15,16},{17,18},{19... | collective-permute-start | bytes 3932168 | tf_op jit(solution)/shard_map/ppermute | solution.py:266
  5.2 3.1 %copy-start.4 = (f32[8]{0:T(128)S(1)}, f32[8]{0:T(128)}, u32[]{:S(2)}) copy-start(f32[8]{0:T(128)} %param.10) | copy-start | bytes 100
  5.2 3.1 %copy-start.5 = (f32[8]{0:T(128)S(1)}, f32[8]{0:T(128)}, u32[]{:S(2)}) copy-start(f32[8]{0:T(128)} %param.9) | copy-start | bytes 100
  6.5 3.4 %collective-permute-start = (f32[3,256,256]{2,1,0:T(8,128)S(1)}, f32[3,256,256]{2,1,0:T(8,128)S(1)}, u32[]{:S(2)}, u32[]{:S(2)}) collective-permute-start(f32[3,256,256]{2,1,0:T(8,128)S(1)} %slice_bitcast_fusion.refs_0_), channel_id=1, source_target_pairs={{0,1},{1,0},{2,3},{3,2},{4,5},{5,4},{6,7},{7,6},{8,9},{9,8},{10,11... | collective-permute-start | bytes 2359304 | tf_op jit(solution)/shard_map/ppermute | solution.py:266
  7.7 2.2 %collective-permute-start.1 = (f32[2,256,256]{2,1,0:T(8,128)S(1)}, f32[2,256,256]{2,1,0:T(8,128)}, u32[]{:S(2)}, u32[]{:S(2)}) collective-permute-start(f32[2,256,256]{2,1,0:T(8,128)S(1)} %slice_bitcast_fusion.1.refs_2_.refs_1_), channel_id=1, source_target_pairs={{0,1},{1,0},{2,3},{3,2},{4,5},{5,4},{6,7},{7,6},{8,9},{9,8},{10,11... | collective-permute-start | bytes 1572872 | tf_op jit(solution)/shard_map/ppermute | solution.py:266
  9.9 1.0 %copy-start.3 = (f32[1,256,256]{2,1,0:T(8,128)S(1)}, f32[1,256,256]{2,1,0:T(8,128)}, u32[]{:S(2)}) copy-start(f32[1,256,256]{2,1,0:T(8,128)} %param.8) | copy-start | bytes 786436
  13.3 21.5 %collective-permute-start.5 = (f32[2560,128]{1,0:T(8,128)S(1)}, f32[2560,128]{1,0:T(8,128)S(1)}, u32[]{:S(2)}, u32[]{:S(2)}) collective-permute-start(f32[2560,128]{1,0:T(8,128)S(1)} %get-tuple-element.17), channel_id=1, source_target_pairs={{1,2},{3,4},{5,6},{7,8},{9,10},{11,12},{13,14},{15,16},{17,18},{19... | collective-permute-start | bytes 3932168 | tf_op jit(solution)/shard_map/ppermute | solution.py:266
  21.5 3.1 %collective-permute-start.3 = (f32[3,256,256]{2,1,0:T(8,128)S(1)}, f32[3,256,256]{2,1,0:T(8,128)S(1)}, u32[]{:S(2)}, u32[]{:S(2)}) collective-permute-start(f32[3,256,256]{2,1,0:T(8,128)S(1)} %get-tuple-element.15.refs_0_), channel_id=1, source_target_pairs={{0,1},{1,0},{2,3},{3,2},{4,5},{5,4},{6,7},{7,6},{8,9},{9,8},{10,11... | collective-permute-start | bytes 2359304 | tf_op jit(solution)/shard_map/ppermute | solution.py:266
  21.6 3.0 %collective-permute-start.4 = (f32[2,256,256]{2,1,0:T(8,128)S(1)}, f32[2,256,256]{2,1,0:T(8,128)S(1)}, u32[]{:S(2)}, u32[]{:S(2)}) collective-permute-start(f32[2,256,256]{2,1,0:T(8,128)S(1)} %get-tuple-element.16.refs_2_), channel_id=1, source_target_pairs={{0,1},{1,0},{2,3},{3,2},{4,5},{5,4},{6,7},{7,6},{8,9},{9,8},{10,11... | collective-permute-start | bytes 1572872 | tf_op jit(solution)/shard_map/ppermute | solution.py:266
  34.8 54.0 %copy-start.1 = (f32[10,128,1,256]{3,2,1,0:T(1,128)S(1)}, f32[10,128,1,256]{3,2,1,0:T(1,128)}, u32[]{:S(2)}) copy-start(f32[10,128,1,256]{3,2,1,0:T(1,128)} %param.11) | copy-start | bytes 3932164
  34.8 54.0 %copy-start.2 = (f32[10,128,1,256]{3,2,1,0:T(1,128)S(1)}, f32[10,128,1,256]{3,2,1,0:T(1,128)}, u32[]{:S(2)}) copy-start(f32[10,128,1,256]{3,2,1,0:T(1,128)} %param.12) | copy-start | bytes 3932164
  34.9 53.8 %copy-start = (f32[16,128,1,256]{3,2,1,0:T(1,128)S(1)}, f32[16,128,1,256]{3,2,1,0:T(1,128)}, u32[]{:S(2)}) copy-start(f32[16,128,1,256]{3,2,1,0:T(1,128)} %param.13) | copy-start | bytes 6291460
